TPU v7x, 128 devices: a whole 4x4x4 slice. The times are simulated.
128 devices in a mesh: fsdp: 8 (over z, x_hi), ctx: 16 (over x_lo, y, core).
Axes of the slice: x: 4 (x_hi: 2, x_lo: 2; x = x_hi * 2 + x_lo), y: 4, z: 4, core: 2. Of those that a mesh axis runs over, the one named last changes fastest.
Arguments:
- hidden_in: bfloat16 [8, 2048, 2048], P('fsdp', 'ctx'), may hold values from -6 to 6
- out_grad: bfloat16 [8, 2048, 2048], P('fsdp', 'ctx'), may hold values from -6 to 6
- positions: int32 [8, 2048], P('fsdp', 'ctx'), may hold values from 0 to 6142, as said below
- documents: int32 [8, 2048], P('fsdp', 'ctx'), may hold values from 0 to 1, as said below
- qkv_weight: float32 [2048, 6144], P(('fsdp', 'ctx')), may hold values from -0.125 to 0.125
- qkv_first: float32 [2048, 6144], P(('fsdp', 'ctx')), may hold values from -80 to 80
- qkv_second: float32 [2048, 6144], P(('fsdp', 'ctx')), may hold values from 983.04 to 3276.8
- out_weight: float32 [2048, 2048], P(('fsdp', 'ctx')), may hold values from -0.5 to 0.5
- out_first: float32 [2048, 2048], P(('fsdp', 'ctx')), may hold values from -28 to 28
- out_second: float32 [2048, 2048], P(('fsdp', 'ctx')), may hold values from 117.9648 to 393.216
- gate_weight: float32 [2048, 5632], P(('fsdp', 'ctx')), may hold values from -0.125 to 0.125
- gate_first: float32 [2048, 5632], P(('fsdp', 'ctx')), may hold values from -28 to 28
- gate_second: float32 [2048, 5632], P(('fsdp', 'ctx')), may hold values from 127.7952 to 425.984
- up_weight: float32 [2048, 5632], P(('fsdp', 'ctx')), may hold values from -0.125 to 0.125
- up_first: float32 [2048, 5632], P(('fsdp', 'ctx')), may hold values from -28 to 28
- up_second: float32 [2048, 5632], P(('fsdp', 'ctx')), may hold values from 127.7952 to 425.984
- down_weight: float32 [5632, 2048], P(('fsdp', 'ctx')), may hold values from -0.078125 to 0.078125
- down_first: float32 [5632, 2048], P(('fsdp', 'ctx')), may hold values from -48 to 48
- down_second: float32 [5632, 2048], P(('fsdp', 'ctx')), may hold values from 353.8944 to 1179.648
- small_params: float32 [7, 2048], P(None, ('fsdp', 'ctx')), may hold values from -1 to 1.4, as said below
- small_first: float32 [7, 2048], P(None, ('fsdp', 'ctx')), may hold values from -80 to 80
- small_second: float32 [7, 2048], P(None, ('fsdp', 'ctx')), may hold values from 983.04 to 3276.8
Outputs:
- block_out: bfloat16 [8, 2048, 2048], P('fsdp', 'ctx')
- input_grad: float32 [8, 2048, 2048], P('fsdp', 'ctx')
- qkv_weight_new: float32 [2048, 6144], P(('fsdp', 'ctx'))
- qkv_first_new: float32 [2048, 6144], P(('fsdp', 'ctx'))
- qkv_second_new: float32 [2048, 6144], P(('fsdp', 'ctx'))
- out_weight_new: float32 [2048, 2048], P(('fsdp', 'ctx'))
- out_first_new: float32 [2048, 2048], P(('fsdp', 'ctx'))
- out_second_new: float32 [2048, 2048], P(('fsdp', 'ctx'))
- gate_weight_new: float32 [2048, 5632], P(('fsdp', 'ctx'))
- gate_first_new: float32 [2048, 5632], P(('fsdp', 'ctx'))
- gate_second_new: float32 [2048, 5632], P(('fsdp', 'ctx'))
- up_weight_new: float32 [2048, 5632], P(('fsdp', 'ctx'))
- up_first_new: float32 [2048, 5632], P(('fsdp', 'ctx'))
- up_second_new: float32 [2048, 5632], P(('fsdp', 'ctx'))
- down_weight_new: float32 [5632, 2048], P(('fsdp', 'ctx'))
- down_first_new: float32 [5632, 2048], P(('fsdp', 'ctx'))
- down_second_new: float32 [5632, 2048], P(('fsdp', 'ctx'))
- small_params_new: float32 [7, 2048], P(None, ('fsdp', 'ctx'))
- small_first_new: float32 [7, 2048], P(None, ('fsdp', 'ctx'))
- small_second_new: float32 [7, 2048], P(None, ('fsdp', 'ctx'))
Inputs may be any that keep to these rules, and one draw needn't show every extreme that they name: `documents`: each sequence holds document 0 on its first 1 to 127 positions and document 1 on all the rest. Within a document the positions rise by one; document 0 starts at a position below 4096, and document 1 ends at position 6142 in every sequence. `small_params`: gains lie in 0.6 to 1.4, shifts and biases in -1 to 1.
All inputs are finite; a program needn't handle non-finite values.
Results may differ from a plain program's by a relative error of at most 0.039.
Values may be sent and summed in bfloat16 or wider, within the bound.
A program may use at most 512 MiB of HBM per device.

v0:
```python
import math

import jax
import jax.numpy as jnp
from jax import lax
from jax.sharding import PartitionSpec as P

D = 2048
H = 32
HEAD = 64
FF = 5632
ROT = 16
STEP = 10


NORM_EPS = 1e-05
BETA_ONE = 0.9
BETA_TWO = 0.95
ADAM_EPS = 1e-08
MASKED = -1e30


def side_by_side(arrays, axis, dim, along):
    widths = [a.shape[along] for a in arrays]
    both = jnp.concatenate(arrays, axis=along)
    whole = lax.all_gather(both, axis, axis=dim, tiled=True)
    return tuple(jnp.split(whole, [sum(widths[:k]) for k in range(1, len(widths))], axis=along))


def in_one_piece(arrays, axis, dim, along):
    widths = [math.prod(a.shape[along:]) for a in arrays]
    both = jnp.concatenate(
        [a.reshape(*a.shape[:along], w) for a, w in zip(arrays, widths)], axis=along
    )
    whole = lax.all_gather(both, axis, axis=dim, tiled=True)
    pieces = jnp.split(whole, [sum(widths[:k]) for k in range(1, len(widths))], axis=along)
    return tuple(
        (b.reshape(*whole.shape[:along], *a.shape[along:]) for a, b in zip(arrays, pieces))
    )


def sent_together(arrays, axis, dim, along):
    ends, at = ([], 0)
    for a in arrays[:-1]:
        at += a.shape[along]
        ends.append(at)
    both = jnp.concatenate(arrays, axis=along)
    return tuple(
        jnp.split(lax.psum_scatter(both, axis, scatter_dimension=dim, tiled=True), ends, axis=along)
    )


def side_by_side_2(arrays, axis, dim, along):
    widths = [math.prod(a.shape[along:]) for a in arrays]
    both = jnp.concatenate(
        [a.reshape(*a.shape[:along], w) for a, w in zip(arrays, widths)], axis=along
    )
    whole = lax.psum_scatter(both, axis, scatter_dimension=dim, tiled=True)
    pieces = jnp.split(whole, [sum(widths[:k]) for k in range(1, len(widths))], axis=along)
    return tuple(
        (b.reshape(*whole.shape[:along], *a.shape[along:]) for a, b in zip(arrays, pieces))
    )


def norm_forward(rows, gain, shift):
    mean = jnp.mean(rows, axis=-1, keepdims=True)
    centred = rows - mean
    scale = lax.rsqrt(jnp.mean(centred * centred, axis=-1, keepdims=True) + NORM_EPS)
    unit = centred * scale
    return (unit * gain + shift, unit, scale)


def norm_backward(gradient, unit, scale, gain):
    along = gradient * gain
    inner = (
        along
        - jnp.mean(along, axis=-1, keepdims=True)
        - unit * jnp.mean(along * unit, axis=-1, keepdims=True)
    )
    return (inner * scale, jnp.sum(gradient * unit, axis=0), jnp.sum(gradient, axis=0))


def rotary(heads, positions, sign):
    half = ROT // 2
    freq = 10000.0 ** (-jnp.arange(half).astype(jnp.float32) / half)
    angle = positions.astype(jnp.float32)[..., None] * freq
    cosine = jnp.cos(angle)[..., None, :]
    sine = sign * jnp.sin(angle)[..., None, :]
    first = heads[..., :half]
    second = heads[..., half:ROT]
    return jnp.concatenate(
        [first * cosine - second * sine, second * cosine + first * sine, heads[..., ROT:]], axis=-1
    )


def adamw(weight, first, second, gradient, rate, decay):
    first_new = BETA_ONE * first + (1.0 - BETA_ONE) * gradient
    second_new = BETA_TWO * second + (1.0 - BETA_TWO) * gradient * gradient
    mean_hat = first_new / (1.0 - BETA_ONE**STEP)
    square_hat = second_new / (1.0 - BETA_TWO**STEP)
    weight_new = weight - rate * (mean_hat / (jnp.sqrt(square_hat) + ADAM_EPS) + decay * weight)
    return (weight_new, first_new, second_new)


def block_size(count):
    return math.gcd(count, 512)


def split_keys(array, size):
    shape = array.shape
    blocks = array.reshape((shape[0], shape[1] // size, size) + shape[2:])
    return jnp.moveaxis(blocks, 1, 0)


def local(
    hidden_in,
    out_grad,
    positions,
    documents,
    qkv_weight,
    qkv_first,
    qkv_second,
    out_weight,
    out_first,
    out_second,
    gate_weight,
    gate_first,
    gate_second,
    up_weight,
    up_first,
    up_second,
    down_weight,
    down_first,
    down_second,
    small_params,
    small_first,
    small_second,
):
    seq_count, block_len, width = hidden_in.shape
    row_count = seq_count * block_len
    qkv_low = qkv_weight.astype(jnp.bfloat16)
    out_low = out_weight.astype(jnp.bfloat16)
    gate_low = gate_weight.astype(jnp.bfloat16)
    up_low = up_weight.astype(jnp.bfloat16)
    down_low = down_weight.astype(jnp.bfloat16)
    small_low = small_params.astype(jnp.bfloat16)
    w_qkv, w_out, w_gate, w_up, w_down, small_all = (
        *side_by_side((qkv_low, out_low, gate_low, up_low), ("fsdp", "ctx"), 0, 1),
        lax.all_gather(down_low, ("fsdp", "ctx"), axis=0, tiled=True),
        lax.all_gather(small_low, ("fsdp", "ctx"), axis=1, tiled=True),
    )
    params = small_all.astype(jnp.float32)
    rows = hidden_in.reshape(row_count, width).astype(jnp.float32)
    normed, unit_one, scale_one = norm_forward(rows, params[0], params[1])
    normed_low = normed.astype(jnp.bfloat16)
    mixed = jnp.dot(normed_low, w_qkv, preferred_element_type=jnp.float32) + params[2:5].reshape(
        3 * width
    )
    heads = mixed.reshape(seq_count, block_len, 3, H, HEAD)
    query = rotary(heads[:, :, 0], positions, 1.0).astype(jnp.bfloat16)
    key = rotary(heads[:, :, 1], positions, 1.0).astype(jnp.bfloat16)
    value = heads[:, :, 2].astype(jnp.bfloat16)
    key_marks = documents.astype(jnp.bfloat16)
    query_marks = documents.astype(jnp.float32)
    place = lax.axis_index("ctx") * block_len
    query_rows = place + jnp.arange(block_len)
    factor = HEAD ** (-0.5)

    def key_scores(keys, key_ids, start):
        count = keys.shape[1]
        scores = (
            jnp.einsum("sqhd,skhd->sqhk", query, keys, preferred_element_type=jnp.float32) * factor
        )
        key_rows = start + jnp.arange(count)
        allowed = (key_rows[None, None, :] <= query_rows[None, :, None]) & (
            key_ids.astype(jnp.float32)[:, None, :] == query_marks[:, :, None]
        )
        allowed = allowed[:, :, None, :]
        return (jnp.where(allowed, scores, MASKED), allowed)

    start_state = (
        jnp.full((seq_count, block_len, H), MASKED, jnp.float32),
        jnp.zeros((seq_count, block_len, H), jnp.float32),
        jnp.zeros((seq_count, block_len, H, HEAD), jnp.float32),
    )
    piece = in_one_piece((key, value, key_marks), "ctx", 1, 2)
    size = block_size(piece[0].shape[1])

    def one_block(state, inner):
        keys, values, key_ids, offset = inner

        def update(current):
            running, total, weighted = current
            scores, allowed = key_scores(keys, key_ids, offset)
            highest = jnp.maximum(running, jnp.max(scores, axis=-1))
            weights = jnp.where(allowed, jnp.exp(scores - highest[..., None]), 0.0)
            shrink = jnp.exp(running - highest)
            part = jnp.einsum(
                "sqhk,skhd->sqhd",
                weights.astype(jnp.bfloat16),
                values,
                preferred_element_type=jnp.float32,
            )
            return (
                highest,
                total * shrink + jnp.sum(weights, axis=-1),
                weighted * shrink[..., None] + part,
            )

        def keep_state(current):
            return current

        return (lax.cond(offset > place + block_len - 1, keep_state, update, state), None)

    offsets = size * jnp.arange(piece[0].shape[1] // size)
    result, unused = lax.scan(
        one_block,
        start_state,
        (
            split_keys(piece[0], size),
            split_keys(piece[1], size),
            split_keys(piece[2], size),
            offsets,
        ),
    )
    running, total, weighted = result
    attended = weighted / total[..., None]
    log_total = running + jnp.log(total)
    attended_low = attended.reshape(row_count, width).astype(jnp.bfloat16)
    branch = jnp.dot(attended_low, w_out, preferred_element_type=jnp.float32)
    middle = rows + branch
    normed_two, unit_two, scale_two = norm_forward(middle, params[5], params[6])
    normed_two_low = normed_two.astype(jnp.bfloat16)
    gate = jnp.dot(normed_two_low, w_gate, preferred_element_type=jnp.float32)
    up = jnp.dot(normed_two_low, w_up, preferred_element_type=jnp.float32)
    sigmoid_gate = jax.nn.sigmoid(gate)
    activated = gate * sigmoid_gate
    hidden_low = (activated * up).astype(jnp.bfloat16)
    result = middle + jnp.dot(hidden_low, w_down, preferred_element_type=jnp.float32)
    block_out = result.reshape(seq_count, block_len, width).astype(jnp.bfloat16)
    w_qkv, w_out, w_gate, w_up, w_down, small_all = (
        *side_by_side((qkv_low, out_low, gate_low, up_low), ("fsdp", "ctx"), 0, 1),
        lax.all_gather(down_low, ("fsdp", "ctx"), axis=0, tiled=True),
        lax.all_gather(small_low, ("fsdp", "ctx"), axis=1, tiled=True),
    )
    params = small_all.astype(jnp.float32)
    outer = out_grad.reshape(row_count, width)
    d_down = jnp.einsum("tf,td->fd", hidden_low, outer, preferred_element_type=jnp.float32)
    d_hidden = jnp.einsum("td,fd->tf", outer, w_down, preferred_element_type=jnp.float32)
    d_up_low = (d_hidden * activated).astype(jnp.bfloat16)
    d_gate_low = (d_hidden * up * sigmoid_gate * (1.0 + gate * (1.0 - sigmoid_gate))).astype(
        jnp.bfloat16
    )
    d_gate = jnp.einsum("td,tf->df", normed_two_low, d_gate_low, preferred_element_type=jnp.float32)
    d_up = jnp.einsum("td,tf->df", normed_two_low, d_up_low, preferred_element_type=jnp.float32)
    d_normed_two = jnp.einsum(
        "tf,df->td", d_gate_low, w_gate, preferred_element_type=jnp.float32
    ) + jnp.einsum("tf,df->td", d_up_low, w_up, preferred_element_type=jnp.float32)
    d_middle_part, d_gain_two, d_shift_two = norm_backward(
        d_normed_two, unit_two, scale_two, params[5]
    )
    d_middle = outer.astype(jnp.float32) + d_middle_part
    d_middle_low = d_middle.astype(jnp.bfloat16)
    d_out = jnp.einsum("td,te->de", attended_low, d_middle_low, preferred_element_type=jnp.float32)
    d_attended = jnp.einsum(
        "te,de->td", d_middle_low, w_out, preferred_element_type=jnp.float32
    ).astype(jnp.bfloat16)
    d_attended = d_attended.reshape(seq_count, block_len, H, HEAD)
    delta = jnp.sum(d_attended.astype(jnp.float32) * attended, axis=-1)
    keys_all, values_all, marks_all = in_one_piece((key, value, key_marks), "ctx", 1, 2)
    size = block_size(keys_all.shape[1])

    def revisit(d_query, inner):
        keys, values, key_ids, offset = inner
        scores, allowed = key_scores(keys, key_ids, offset)
        probs = jnp.where(allowed, jnp.exp(scores - log_total[..., None]), 0.0)
        pulled = jnp.einsum(
            "sqhd,skhd->sqhk", d_attended, values, preferred_element_type=jnp.float32
        )
        d_scores = (probs * (pulled - delta[..., None])).astype(jnp.bfloat16)
        d_query = (
            d_query
            + jnp.einsum("sqhk,skhd->sqhd", d_scores, keys, preferred_element_type=jnp.float32)
            * factor
        )
        key_part = (
            jnp.einsum("sqhk,sqhd->skhd", d_scores, query, preferred_element_type=jnp.float32)
            * factor
        )
        value_part = jnp.einsum(
            "sqhk,sqhd->skhd",
            probs.astype(jnp.bfloat16),
            d_attended,
            preferred_element_type=jnp.float32,
        )
        return (d_query, (key_part, value_part))

    offsets = size * jnp.arange(keys_all.shape[1] // size)
    d_query, key_terms = lax.scan(
        revisit,
        jnp.zeros((seq_count, block_len, H, HEAD), jnp.float32),
        (
            split_keys(keys_all, size),
            split_keys(values_all, size),
            split_keys(marks_all, size),
            offsets,
        ),
    )
    key_total = jnp.moveaxis(key_terms[0], 0, 1).reshape(seq_count, keys_all.shape[1], H, HEAD)
    value_total = jnp.moveaxis(key_terms[1], 0, 1).reshape(seq_count, keys_all.shape[1], H, HEAD)
    d_keys, d_values = tuple(
        (
            part.astype(jnp.float32)
            for part in sent_together(
                (key_total.astype(jnp.bfloat16), value_total.astype(jnp.bfloat16)), "ctx", 1, 0
            )
        )
    )
    d_mixed = jnp.stack(
        [rotary(d_query, positions, -1.0), rotary(d_keys, positions, -1.0), d_values], axis=2
    )
    d_mixed_low = d_mixed.reshape(row_count, 3 * width).astype(jnp.bfloat16)
    d_qkv = jnp.einsum("td,te->de", normed_low, d_mixed_low, preferred_element_type=jnp.float32)
    d_bias = jnp.sum(d_mixed_low.astype(jnp.float32), axis=0)
    d_normed = jnp.einsum("te,de->td", d_mixed_low, w_qkv, preferred_element_type=jnp.float32)
    d_rows_part, d_gain_one, d_shift_one = norm_backward(d_normed, unit_one, scale_one, params[0])
    input_grad = (d_middle + d_rows_part).reshape(seq_count, block_len, width)
    d_small = jnp.concatenate(
        [
            d_gain_one[None],
            d_shift_one[None],
            d_bias.reshape(3, width),
            d_gain_two[None],
            d_shift_two[None],
        ],
        axis=0,
    )
    shard_count = lax.axis_size("fsdp")
    block_count = lax.axis_size("ctx")
    owners = shard_count * block_count

    def spread(array):
        return array.reshape(shard_count, block_count, array.shape[0] // owners, array.shape[1])

    small_spread = d_small.reshape(7, shard_count, block_count, width // owners)
    sectioned = (
        lax.psum_scatter(
            spread(d_qkv).astype(jnp.bfloat16), "ctx", scatter_dimension=1, tiled=True
        ).astype(jnp.float32),
        lax.psum_scatter(
            spread(d_out).astype(jnp.bfloat16), "ctx", scatter_dimension=1, tiled=True
        ).astype(jnp.float32),
        lax.psum_scatter(
            spread(d_gate).astype(jnp.bfloat16), "ctx", scatter_dimension=1, tiled=True
        ).astype(jnp.float32),
        lax.psum_scatter(
            spread(d_up).astype(jnp.bfloat16), "ctx", scatter_dimension=1, tiled=True
        ).astype(jnp.float32),
        lax.psum_scatter(
            spread(d_down).astype(jnp.bfloat16), "ctx", scatter_dimension=1, tiled=True
        ).astype(jnp.float32),
        lax.psum_scatter(
            small_spread.astype(jnp.bfloat16), "ctx", scatter_dimension=2, tiled=True
        ).astype(jnp.float32),
    )
    reduced = (
        *tuple(
            (
                part.astype(jnp.float32)
                for part in side_by_side_2(
                    (
                        sectioned[0].astype(jnp.bfloat16),
                        sectioned[1].astype(jnp.bfloat16),
                        sectioned[2].astype(jnp.bfloat16),
                        sectioned[3].astype(jnp.bfloat16),
                        sectioned[4].astype(jnp.bfloat16),
                    ),
                    "fsdp",
                    0,
                    2,
                )
            )
        ),
        lax.psum_scatter(
            sectioned[5].astype(jnp.bfloat16), "fsdp", scatter_dimension=1, tiled=True
        ).astype(jnp.float32),
    )
    g_qkv = reduced[0].reshape(qkv_weight.shape)
    g_out = reduced[1].reshape(out_weight.shape)
    g_gate = reduced[2].reshape(gate_weight.shape)
    g_up = reduced[3].reshape(up_weight.shape)
    g_down = reduced[4].reshape(down_weight.shape)
    g_small = reduced[5].reshape(small_params.shape)
    qkv_new = adamw(qkv_weight, qkv_first, qkv_second, g_qkv, D ** (-0.5), 0.1)
    out_new = adamw(out_weight, out_first, out_second, g_out, (D // 16) ** (-0.5), 0.1)
    gate_new = adamw(gate_weight, gate_first, gate_second, g_gate, D ** (-0.5), 0.1)
    up_new = adamw(up_weight, up_first, up_second, g_up, D ** (-0.5), 0.1)
    down_new = adamw(down_weight, down_first, down_second, g_down, FF ** (-0.5), 0.1)
    small_new = adamw(small_params, small_first, small_second, g_small, 2.0, 0.0)
    return (
        block_out,
        input_grad,
        qkv_new[0],
        qkv_new[1],
        qkv_new[2],
        out_new[0],
        out_new[1],
        out_new[2],
        gate_new[0],
        gate_new[1],
        gate_new[2],
        up_new[0],
        up_new[1],
        up_new[2],
        down_new[0],
        down_new[1],
        down_new[2],
        small_new[0],
        small_new[1],
        small_new[2],
    )


def solution(mesh):
    in_specs = (
        P("fsdp", "ctx", None),
        P("fsdp", "ctx", None),
        P("fsdp", "ctx"),
        P("fsdp", "ctx"),
        P(("fsdp", "ctx"), None),
        P(("fsdp", "ctx"), None),
        P(("fsdp", "ctx"), None),
        P(("fsdp", "ctx"), None),
        P(("fsdp", "ctx"), None),
        P(("fsdp", "ctx"), None),
        P(("fsdp", "ctx"), None),
        P(("fsdp", "ctx"), None),
        P(("fsdp", "ctx"), None),
        P(("fsdp", "ctx"), None),
        P(("fsdp", "ctx"), None),
        P(("fsdp", "ctx"), None),
        P(("fsdp", "ctx"), None),
        P(("fsdp", "ctx"), None),
        P(("fsdp", "ctx"), None),
        P(None, ("fsdp", "ctx")),
        P(None, ("fsdp", "ctx")),
        P(None, ("fsdp", "ctx")),
    )
    out_specs = (
        P("fsdp", "ctx", None),
        P("fsdp", "ctx", None),
        P(("fsdp", "ctx"), None),
        P(("fsdp", "ctx"), None),
        P(("fsdp", "ctx"), None),
        P(("fsdp", "ctx"), None),
        P(("fsdp", "ctx"), None),
        P(("fsdp", "ctx"), None),
        P(("fsdp", "ctx"), None),
        P(("fsdp", "ctx"), None),
        P(("fsdp", "ctx"), None),
        P(("fsdp", "ctx"), None),
        P(("fsdp", "ctx"), None),
        P(("fsdp", "ctx"), None),
        P(("fsdp", "ctx"), None),
        P(("fsdp", "ctx"), None),
        P(("fsdp", "ctx"), None),
        P(None, ("fsdp", "ctx")),
        P(None, ("fsdp", "ctx")),
        P(None, ("fsdp", "ctx")),
    )
    return jax.shard_map(local, mesh=mesh, in_specs=in_specs, out_specs=out_specs, check_vma=False)
```

profile of v0, /device:TPU:25, one launch (start us, length us, event | category | flops | bytes accessed | tf_op | source)
XLA Modules:
  0.0 2240.8 jit_solution(276918312840798754)
XLA Ops:
  14.7 37.4 %all-gather = bf16[128,16,7]{1,2,0:T(8,128)(2,1)S(1)} all-gather(bf16[1,16,7]{1,2,0:T(8,128)(2,1)S(1)} %convert_bitcast_fusion.4), channel_id=1, replica_groups=mesh['fsdp'=8,'ctx'=16] {'fsdp','ctx'}, dimensions={0}, use_global_device_ids=true | all-gather | bytes 28896 | tf_op jit(solution)/shard_map/all_gather | solution.py:150
  54.0 147.8 %all-gather.6.cloned.1.call-done = bf16[2048,19456]{1,0:T(8,128)(2,1)} async-done(((bf16[16,19456]{1,0:T(8,128)(2,1)}), bf16[2048,19456]{1,0:T(8,128)(2,1)}) %all-gather.6.cloned.1.call-update) | async-done | bytes 79691792 | tf_op jit(solution)/shard_map/all_gather | solution.py:26
  201.7 11.8 fusion.93
  218.8 78.8 %all-gather.10.cloned.1.call-done = bf16[128,44,2048]{2,1,0:T(8,128)(2,1)} async-done(((bf16[1,44,2048]{2,1,0:T(8,128)(2,1)}), bf16[128,44,2048]{2,1,0:T(8,128)(2,1)}) %all-gather.10.cloned.1.call-update) | async-done | bytes 23068688 | tf_op jit(solution)/shard_map/all_gather | solution.py:149
  297.6 28.2 %reshape.772 = bf16[5632,2048]{1,0:T(8,128)(2,1)} reshape(bf16[128,44,2048]{2,1,0:T(8,128)(2,1)} %all-gather.10.cloned.1.call-done) | data formatting | bytes 46137344
  325.8 13.8 fusion.130
  340.8 55.9 %all-gather.8.cloned.1.call-done = bf16[1,2048,4097]{1,2,0:T(8,128)(2,1)} async-done(((bf16[1,128,4097]{1,2,0:T(8,128)(2,1)}), bf16[1,2048,4097]{1,2,0:T(8,128)(2,1)}) %all-gather.8.cloned.1.call-update) | async-done | bytes 16781328 | tf_op jit(solution)/shard_map/all_gather | solution.py:35
  396.7 11.8 fusion.160
  408.5 14.6 transpose_reshape_reshape.14
  423.1 8.7 copy.102
  431.8 14.6 transpose_reshape_reshape.13
  446.4 8.7 copy.101
  455.9 27.5 %while.32 = (s32[]{:T(128)}, f32[1,128,32]{1,2,0:T(8,128)S(1)}, f32[1,128,32]{1,2,0:T(8,128)S(1)}, f32[1,128,32,64]{1,3,2,0:T(8,128)S(1)}, s32[4]{0:T(128)S(1)},...) while((s32[]{:T(128)}, f32[1,128,32]{1,2,0:T(8,128)S(1)}, ...), condition=%wide.region_7.8_spmd.clone, body=%wide.region_2.7_spmd.clone.sunk | while | flops 564868224 | bytes 32518972 | solution.py:216
  457.4 11.0 conditional.3
  458.3 3.5 fusion.4
  461.9 4.4 fusion.21
  469.7 11.0 conditional.3
  470.6 3.5 fusion.4
  474.2 4.4 fusion.21
  484.4 4.9 fusion.164
  489.9 9.5 fusion.83
  499.4 12.6 multiply_convert_fusion.1
  512.0 12.6 fusion.81
  524.7 13.5 multiply_reduce_fusion
  540.1 7.1 fusion.107
  550.0 78.2 %while.33 = (s32[]{:T(128)}, f32[1,128,32,64]{1,3,2,0:T(8,128)S(1)}, bf16[4,1,512,32,64]{2,4,3,1,0:T(8,128)(2,1)}, bf16[4,1,512,32,64]{2,4,3,1,0:T(8,128)(2,1)},...) while((s32[]{:T(128)}, ...), condition=%wide.region_14.15_spmd.clone, body=%wide.region_13.14_spmd.clone.sunk | while | flops 1369375872 | bytes 56879824 | solution.py:299
  554.6 5.1 fusion.207
  559.7 3.9 bitcast_dynamic-update-slice_fusion.5
  574.0 5.1 fusion.207
  579.1 4.0 bitcast_dynamic-update-slice_fusion.5
  593.5 5.1 fusion.207
  598.7 4.0 bitcast_dynamic-update-slice_fusion.5
  613.0 5.1 fusion.207
  618.2 4.0 bitcast_dynamic-update-slice_fusion.5
  622.2 3.0 fusion.208
  628.1 8.0 copy.138
  636.2 7.9 copy.137
  644.1 13.8 pad_maximum_fusion
  657.9 45.9 %copy.123 = bf16[2,2048,32,64]{3,2,0,1:T(8,128)(2,1)} copy(bf16[2,2048,32,64]{1,3,2,0:T(8,128)(2,1)} %pad_maximum_fusion) | data formatting | bytes 33554432
  703.8 44.4 %reshape.784 = bf16[2048,4096]{1,0:T(8,128)(2,1)} reshape(bf16[2048,2,32,64]{3,2,1,0:T(8,128)(2,1)} %bitcast.399) | data formatting | bytes 33554432
  749.3 5.6 convolution_convert_fusion.4
  754.8 10.9 convolution_convert_fusion.1
  765.8 11.0 convolution_convert_fusion
  776.7 91.0 %reduce-scatter.24.cloned.1.call-done = bf16[128,4096]{1,0:T(8,128)(2,1)} async-done(((bf16[2048,4096]{1,0:T(8,128)(2,1)}), bf16[128,4096]{1,0:T(8,128)(2,1)}) %reduce-scatter.24.cloned.1.call-update) | async-done | bytes 1048592
  867.7 4.2 reshape.785
  872.0 3.3 fusion.161
  884.7 13.8 fusion.77
  903.1 12.8 convolution_convert_fusion.2
  916.0 3.5 fusion.96
  923.3 13.0 convolution_convert_fusion.3
  936.3 26.5 %copy.112 = bf16[8,16,44,2048]{3,0,2,1:T(8,128)(2,1)} copy(bf16[8,16,44,2048]{3,2,1,0:T(8,128)(2,1)} %convolution_convert_fusion.3) | data formatting | bytes 46137344 | tf_op jit(solution)/shard_map/convert_element_type | solution.py:360
  965.7 781.1 %all-reduce.13.cloned.1.call-done = (bf16[8,16,16,6144]{3,2,1,0:T(8,128)(2,1)}, bf16[8,16,16,2048]{3,2,1,0:T(8,128)(2,1)}, bf16[8,16,16,5632]{3,2,1,0:T(8,128)(2,1)}, bf16[8,16,16,5632]{3,2,1,0:T(8,128)(2,1)}) async-done(((bf16[8,16,16,6144]{3,2,1,0:T(8,128)(2,1)}, bf16[8,16,16,2048]{3,2,1,0:T(8,128)(2,1)}, bf16[8,16,16,5632]{3,2,1,0:T(8,128)(2,1)}, bf16[8,16,16,5632]{3,2,1,0:T(8,128)(2,1)}), ...) | async-done | bytes 79691792
  1746.8 3.3 constant_dynamic-slice_fusion.4
  1756.9 3.3 constant_dynamic-slice_fusion.2
  1760.2 3.2 constant_dynamic-slice_fusion.1
  1763.4 3.2 reshape.755
  1766.6 3.1 reshape.754
  1776.8 101.2 %reduce-scatter.22.cloned.1.call-done = bf16[8,1,44,2048]{3,0,2,1:T(8,128)(2,1)} async-done(((bf16[8,16,44,2048]{3,0,2,1:T(8,128)(2,1)}), bf16[8,1,44,2048]{3,0,2,1:T(8,128)(2,1)}) %reduce-scatter.22.cloned.1.call-update) | async-done | bytes 1441808 | tf_op jit(solution)/shard_map/reduce_scatter | solution.py:359
  1881.1 13.5 fusion.111
  1896.1 43.5 %reduce-scatter.26.cloned.1.call-done = bf16[7,8,1,16]{3,1,0,2:T(8,128)(2,1)} async-done(((bf16[7,8,16,16]{3,1,0,2:T(8,128)(2,1)}), bf16[7,8,1,16]{3,1,0,2:T(8,128)(2,1)}) %reduce-scatter.26.cloned.1.call-update) | async-done | bytes 1808
  1940.4 36.9 %all-reduce.6 = bf16[7,8,1,16]{3,0,2,1:T(8,128)(2,1)S(1)} all-reduce(bf16[7,8,1,16]{3,0,2,1:T(8,128)(2,1)S(1)} %copy.114), channel_id=10, replica_groups=mesh['fsdp'=8,'ctx'=16] {'fsdp'}, use_global_device_ids=true, to_apply=%region_30.31.clone | all-reduce | flops 896 | bytes 3584
  1978.5 232.8 %all-reduce.11.cloned.1.call-done = bf16[8,1,401408]{2,0,1:T(8,128)(2,1)} async-done(((bf16[8,1,401408]{2,0,1:T(8,128)(2,1)}), bf16[8,1,401408]{2,0,1:T(8,128)(2,1)}) %all-reduce.11.cloned.1.call-update) | async-done | bytes 6422544
  2213.5 3.2 fusion.136
  2216.8 6.8 fusion.139
  (267 shorter events, 123.8 us)
Async XLA Ops:
  7.2 45.5 %copy-start.4 = (bf16[1,128,2048]{2,1,0:T(8,128)(2,1)S(1)}, bf16[1,128,2048]{2,1,0:T(8,128)(2,1)}, u32[]{:S(2)}) copy-start(bf16[1,128,2048]{2,1,0:T(8,128)(2,1)} %param.28) | copy-start | bytes 1572868
  7.2 45.9 %copy-start.42 = (s32[1,128]{1,0:T(1,128)S(1)}, s32[1,128]{1,0:T(1,128)}, u32[]{:S(2)}) copy-start(s32[1,128]{1,0:T(1,128)} %param.30) | copy-start | bytes 1540
  7.2 46.0 %copy-start.43 = (s32[1,128]{1,0:T(1,128)S(1)}, s32[1,128]{1,0:T(1,128)}, u32[]{:S(2)}) copy-start(s32[1,128]{1,0:T(1,128)} %param.31) | copy-start | bytes 1540
  7.2 194.5 %all-gather.6.cloned.1.call-start = ((), (), s32[]{:S(2)}) async-start(), calls=%async_computation.3 | async-start | bytes 80314368 | tf_op jit(solution)/shard_map/all_gather | solution.py:26
  12.2 285.4 %all-gather.10.cloned.1.call-start = ((), (), s32[]{:S(2)}) async-start(), calls=%async_computation.6 | async-start | bytes 25362432 | tf_op jit(solution)/shard_map/all_gather | solution.py:149
  13.9 382.8 %all-gather.8.cloned.1.call-start = ((), (), s32[]{:S(2)}) async-start(), calls=%async_computation.4 | async-start | bytes 17860608 | tf_op jit(solution)/shard_map/all_gather | solution.py:35
  52.8 160.7 %copy-start.34 = (f32[128]{0:T(128)}, f32[128]{0:T(128)S(1)}, u32[]{:S(2)}) copy-start(f32[128]{0:T(128)S(1)} %broadcast_multiply_fusion.6) | copy-start | bytes 1540
  53.2 160.4 %copy-start.40 = (f32[128]{0:T(128)}, f32[128]{0:T(128)S(1)}, u32[]{:S(2)}) copy-start(f32[128]{0:T(128)S(1)} %add_rsqrt_fusion.1) | copy-start | bytes 1540
  53.9 162.5 %copy-start.28 = (f32[128,8]{0,1:T(8,128)}, f32[128,8]{0,1:T(8,128)S(1)}, u32[]{:S(2)}) copy-start(f32[128,8]{0,1:T(8,128)S(1)} %get-tuple-element.639) | copy-start | bytes 12292
  53.9 147.8 %copy-start.26 = (f32[1,2048]{1,0:T(1,128)}, f32[1,2048]{1,0:T(1,128)S(1)}, u32[]{:S(2)}) copy-start(f32[1,2048]{1,0:T(1,128)S(1)} %get-tuple-element.632) | copy-start | bytes 24580
  54.0 159.6 %copy-start.30 = (f32[1,2048]{1,0:T(1,128)}, f32[1,2048]{1,0:T(1,128)S(1)}, u32[]{:S(2)}) copy-start(f32[1,2048]{1,0:T(1,128)S(1)} %get-tuple-element.631) | copy-start | bytes 24580
  216.4 1.0 copy-start.14
  218.6 649.2 %reduce-scatter.24.cloned.1.call-start = ((), (), s32[]{:S(2)}) async-start(), calls=%async_computation.7 | async-start | bytes 17825792
  218.8 106.9 %copy-start.7 = (bf16[1,128,2048]{2,1,0:T(8,128)(2,1)S(1)}, bf16[1,128,2048]{2,1,0:T(8,128)(2,1)}, u32[]{:S(2)}) copy-start(bf16[1,128,2048]{2,1,0:T(8,128)(2,1)} %param.29) | copy-start | bytes 1572868
  455.9 28.5 %copy-start.5 = (bf16[1,128,2048]{2,1,0:T(8,128)(2,1)S(1)}, bf16[1,128,2048]{2,1,0:T(8,128)(2,1)}, u32[]{:S(2)}) copy-start(bf16[1,128,2048]{2,1,0:T(8,128)(2,1)} %param.28) | copy-start | bytes 1572868
  483.4 1.0 copy-start.3
  484.4 5.5 copy-start.15
  489.3 48.9 %copy-start.1 = (f32[128,2048]{1,0:T(8,128)}, f32[128,2048]{1,0:T(8,128)S(1)}, u32[]{:S(2)}) copy-start(f32[128,2048]{1,0:T(8,128)S(1)} %get-tuple-element.643) | copy-start | bytes 3145732
  489.9 9.5 copy-start.9
  489.9 9.5 copy-start.13
  499.4 12.6 copy-start.12
  512.0 12.7 copy-start.22
  540.0 9.9 copy-start
  748.2 1.0 copy-start.16
  748.3 6.6 copy-start.10
  748.3 998.5 %all-reduce.13.cloned.1.call-start = ((), (), s32[]{:S(2)}) async-start(), calls=%async_computation.10 | async-start | bytes 159383552
  748.3 6.5 copy-start.23
  754.8 10.9 copy-start.21
  776.7 104.9 %copy-start.29 = (f32[128,8]{0,1:T(8,128)S(1)}, f32[128,8]{0,1:T(8,128)}, u32[]{:S(2)}) copy-start(f32[128,8]{0,1:T(8,128)} %copy-done.28) | copy-start | bytes 12292
  776.7 104.9 %copy-start.32 = (f32[128,8]{0,1:T(8,128)S(1)}, f32[128,8]{0,1:T(8,128)}, u32[]{:S(2)}) copy-start(f32[128,8]{0,1:T(8,128)} %get-tuple-element.637) | copy-start | bytes 12292
  884.7 13.8 copy-start.6
  884.7 13.8 copy-start.27
  884.7 13.8 copy-start.31
  884.7 13.8 copy-start.35
  884.7 13.8 copy-start.41
  915.9 962.0 %reduce-scatter.22.cloned.1.call-start = ((), (), s32[]{:S(2)}) async-start(), calls=%async_computation.5 | async-start | bytes 24510464 | tf_op jit(solution)/shard_map/reduce_scatter | solution.py:359
  962.9 0.7 copy-start.45
  962.9 1.2 copy-start.37
  962.9 1.3 copy-start.36
  962.9 976.8 %reduce-scatter.26.cloned.1.call-start = ((), (), s32[]{:S(2)}) async-start(), calls=%async_computation.9 | async-start | bytes 243712
  965.4 1245.8 %all-reduce.11.cloned.1.call-start = ((), (), s32[]{:S(2)}) async-start(), calls=%async_computation.8 | async-start | bytes 12845056
  1769.8 5.8 copy-start.8
  1775.6 105.0 %copy-start.44 = (u32[128]{0:T(128)S(1)}, u32[128]{0:T(128)}, u32[]{:S(2)}) copy-start(u32[128]{0:T(128)} %constant.211) | copy-start | bytes 1540
  1775.6 105.6 %copy-start.2 = (f32[128,2048]{1,0:T(8,128)S(1)}, f32[128,2048]{1,0:T(8,128)}, u32[]{:S(2)}) copy-start(f32[128,2048]{1,0:T(8,128)} %copy-done.1) | copy-start | bytes 3145732
  1881.1 13.5 copy-start.11
  1881.1 96.1 %copy-start.33 = (f32[7,16]{1,0:T(8,128)S(1)}, f32[7,16]{1,0:T(8,128)}, u32[]{:S(2)}) copy-start(f32[7,16]{1,0:T(8,128)} %param.47) | copy-start | bytes 1348
  1881.1 96.1 %copy-start.38 = (f32[7,16]{1,0:T(8,128)S(1)}, f32[7,16]{1,0:T(8,128)}, u32[]{:S(2)}) copy-start(f32[7,16]{1,0:T(8,128)} %param.48) | copy-start | bytes 1348
  1881.1 96.1 %copy-start.39 = (f32[7,16]{1,0:T(8,128)S(1)}, f32[7,16]{1,0:T(8,128)}, u32[]{:S(2)}) copy-start(f32[7,16]{1,0:T(8,128)} %param.49) | copy-start | bytes 1348
  1894.7 331.0 %copy-start.19 = (f32[16,5632]{1,0:T(8,128)S(1)}, f32[16,5632]{1,0:T(8,128)}, u32[]{:S(2)}) copy-start(f32[16,5632]{1,0:T(8,128)} %param.38) | copy-start | bytes 1081348
  1896.1 331.8 %copy-start.20 = (f32[16,5632]{1,0:T(8,128)S(1)}, f32[16,5632]{1,0:T(8,128)}, u32[]{:S(2)}) copy-start(f32[16,5632]{1,0:T(8,128)} %param.41) | copy-start | bytes 1081348
  1896.1 334.0 %copy-start.17 = (f32[44,2048]{1,0:T(8,128)S(1)}, f32[44,2048]{1,0:T(8,128)}, u32[]{:S(2)}) copy-start(f32[44,2048]{1,0:T(8,128)} %param.44) | copy-start | bytes 1081348
  2216.8 15.7 copy-start.18
  2223.8 8.7 copy-start.24
  2223.8 8.7 copy-start.25
Sparse Core Ops, SparseCore 0:
  12.3 189.4 all-gather.5
  205.4 92.1 all-gather.9
  299.2 97.4 all-gather.7
  748.4 119.2 reduce-scatter.23
  916.1 830.7 all-reduce.12
  1749.1 128.7 reduce-scatter.21
  1880.9 58.7 reduce-scatter.25
  1942.3 268.8 all-reduce.10
where the time goes:
time: 2250 us; the launch traced here: 2240 us
  waiting for transfers between devices  1530 us (68%)
  local copies, waits for them, and re-layouts  289 us (13%)
  matrix products  254 us (11%)
  blocking collectives  74.2 us (3%)
  other arithmetic  71.8 us (3%)
    unnamed x12, waiting for transfers between devices  1150 us
    unnamed x114, local copies, waits for them, and re-layouts  169 us
    all_gather x1, waiting for transfers between devices, side_by_side(): whole = lax.all_gather(both, axis, axis=dim, tiled=True)  148 us
    reduce_scatter x1, waiting for transfers between devices, local(): lax.psum_scatter(spread(d_down).astype(jnp.bfloat16), 'ctx', scatter_dime...  101 us
    all_gather x1, waiting for transfers between devices, local(): lax.all_gather(down_low, ('fsdp', 'ctx'), axis=0, tiled=True)  78.8 us
    all_gather x1, waiting for transfers between devices, in_one_piece(): whole = lax.all_gather(both, axis, axis=dim, tiled=True)  55.9 us
  transfers between devices with their start and end apart: 8, of which 8 were waited for; matrix products, arithmetic and copies ran while one was open for 8% of the time, Pallas kernels for 0%

commit v1 on v0

v1 whole, which is shorter than its diff:
```python
import functools
import math

import jax
import jax.numpy as jnp
import numpy as np
from jax import lax
from jax.experimental import pallas as pl
from jax.experimental.pallas import tpu as pltpu
from jax.sharding import Mesh
from jax.sharding import PartitionSpec as P

D = 2048
H = 32
HEAD = 64
FF = 5632
ROT = 16
STEP = 10

NORM_EPS = 1e-05
BETA_ONE = 0.9
BETA_TWO = 0.95
ADAM_EPS = 1e-08
MASKED = -1e30

AXES = ("z", "xh", "xl", "y", "core")
YC = ("y", "core")
ZX = ("z", "xh", "xl")
HALF = 1024
SEQ = 2048
BF = jnp.bfloat16
F32 = jnp.float32


def norm_forward(rows, gain, shift):
    mean = jnp.mean(rows, axis=-1, keepdims=True)
    centred = rows - mean
    scale = lax.rsqrt(jnp.mean(centred * centred, axis=-1, keepdims=True) + NORM_EPS)
    unit = centred * scale
    return (unit * gain + shift, unit, scale)


def norm_backward(gradient, unit, scale, gain):
    along = gradient * gain
    inner = (
        along
        - jnp.mean(along, axis=-1, keepdims=True)
        - unit * jnp.mean(along * unit, axis=-1, keepdims=True)
    )
    return (inner * scale, jnp.sum(gradient * unit, axis=0), jnp.sum(gradient, axis=0))


def adamw(weight, first, second, gradient, rate, decay):
    first_new = BETA_ONE * first + (1.0 - BETA_ONE) * gradient
    second_new = BETA_TWO * second + (1.0 - BETA_TWO) * gradient * gradient
    mean_hat = first_new / (1.0 - BETA_ONE**STEP)
    square_hat = second_new / (1.0 - BETA_TWO**STEP)
    weight_new = weight - rate * (mean_hat / (jnp.sqrt(square_hat) + ADAM_EPS) + decay * weight)
    return (weight_new, first_new, second_new)


def dot_nn(a, b):
    return jnp.dot(a, b, preferred_element_type=F32)


def dot_nt(a, b):
    return lax.dot_general(a, b, (((1,), (1,)), ((), ())), preferred_element_type=F32)


def dot_tn(a, b):
    return lax.dot_general(a, b, (((0,), (0,)), ((), ())), preferred_element_type=F32)


def rotary_tables(positions):
    half = ROT // 2
    freq = 10000.0 ** (-jnp.arange(half).astype(F32) / half)
    lane = np.arange(128) % HEAD
    lane_freq = jnp.where(lane < ROT, jnp.tile(freq, 128 // half), 0.0)
    angle = positions.astype(F32)[:, None] * lane_freq[None, :]
    sine = jnp.sin(angle)
    low = jnp.asarray(lane < half)
    return jnp.cos(angle), jnp.where(low, -sine, 0.0), jnp.where(low, 0.0, sine)


def rotate(x, cosine, below, above):
    return x * cosine + pltpu.roll(x, 120, 1) * below + pltpu.roll(x, 8, 1) * above


def remote(src, dst, sems, at, device):
    return pltpu.make_async_remote_copy(
        src_ref=src,
        dst_ref=dst,
        send_sem=sems.at[0, at],
        recv_sem=sems.at[1, at],
        device_id=device,
        device_id_type=pl.DeviceIdType.MESH,
    )


def places():
    y, c, z = lax.axis_index("y"), lax.axis_index("core"), lax.axis_index("z")
    x = lax.axis_index("xh") * 2 + lax.axis_index("xl")
    step = lambda v, k: lax.rem(v + k, 4)
    at_x = lambda v: {"xh": lax.div(v, 2), "xl": lax.rem(v, 2)}
    devices = {
        "twin": {"core": 1 - c},
        "up": {"y": step(y, 1)},
        "down": {"y": step(y, 3)},
        "across": {"y": step(y, 2)},
        "up_twin": {"y": step(y, 1), "core": 1 - c},
        "down_twin": {"y": step(y, 3), "core": 1 - c},
        "across_twin": {"y": step(y, 2), "core": 1 - c},
        "x+": at_x(step(x, 1)),
        "x-": at_x(step(x, 3)),
        "z+": {"z": step(z, 1)},
        "z-": {"z": step(z, 3)},
        "pair": {"xl": 1 - lax.axis_index("xl")},
    }
    return y, c, x, z, devices


def add_low(a, b):
    return (a.astype(F32) + b.astype(F32)).astype(BF)


def ring_gather(block, cut, i, plus, minus, sems, base, pending):
    before, after = lax.rem(i + 3, 4), lax.rem(i + 1, 4)
    to_plus = remote(block(i), block(i), sems, base, plus)
    to_minus = remote(block(i), block(i), sems, base + 1, minus)
    to_plus.start()
    to_minus.start()
    yield
    to_plus.wait_recv()
    lo = cut(block(before))[0]
    pass_plus = remote(lo, lo, sems, base + 2, plus)
    pass_plus.start()
    yield
    to_minus.wait_recv()
    hi = cut(block(after))[1]
    pass_minus = remote(hi, hi, sems, base + 3, minus)
    pass_minus.start()
    pending += [to_plus, to_minus, pass_plus, pass_minus]
    yield
    pass_plus.wait_recv()
    pass_minus.wait_recv()


def ring_scatter(block, cut, i, plus, minus, acc, near, sems, base, pending):
    before, after, across = lax.rem(i + 3, 4), lax.rem(i + 1, 4), lax.rem(i + 2, 4)
    lo, hi = (lambda v: cut(v)[0]), (lambda v: cut(v)[1])
    far_plus = remote(lo(block(across)), lo(near.at[0]), sems, base, plus)
    far_minus = remote(hi(block(across)), hi(near.at[0]), sems, base + 1, minus)
    own_plus = remote(hi(block(after)), hi(near.at[1]), sems, base + 2, plus)
    own_minus = remote(lo(block(before)), lo(near.at[2]), sems, base + 3, minus)
    for copy in (far_plus, far_minus, own_plus, own_minus):
        copy.start()
    yield
    far_plus.wait_recv()
    lo(acc)[...] = add_low(lo(block(after))[...], lo(near.at[0])[...])
    sum_plus = remote(lo(acc), lo(near.at[1]), sems, base + 4, plus)
    sum_plus.start()
    yield
    far_minus.wait_recv()
    hi(acc)[...] = add_low(hi(block(before))[...], hi(near.at[0])[...])
    sum_minus = remote(hi(acc), hi(near.at[2]), sems, base + 5, minus)
    sum_minus.start()
    pending += [far_plus, far_minus, own_plus, own_minus, sum_plus, sum_minus]
    yield
    for copy in (own_plus, own_minus, sum_plus, sum_minus):
        copy.wait_recv()


class GatherTokens:
    peers = ("twin", "up", "down")
    n_sems = 10

    def __init__(self, rows, width):
        self.ins = [((rows, width), BF)]
        self.outs = [((8, rows, width), BF)]
        self.scratch = []
        self.rows = rows

    def run(self, ins, outs, scratch, sems, base, place, pending):
        y, c, _, _, to = place
        (x_ref,), (out_ref,) = ins, outs
        half = self.rows // 2
        lo, hi = pl.ds(0, half), pl.ds(half, half)
        at = lambda k: lax.rem(y + k, 4) * 2 + c
        mine = pltpu.make_async_copy(x_ref, out_ref.at[at(0)], sems.at[0, base + 9])
        s_up = remote(x_ref, out_ref.at[at(0)], sems, base, to["up"])
        s_down = remote(x_ref, out_ref.at[at(0)], sems, base + 1, to["down"])
        s_twin = remote(x_ref, out_ref.at[at(0)], sems, base + 2, to["twin"])
        for copy in (s_up, s_down, s_twin, mine):
            copy.start()
        pass_on = lambda ref, k, device: remote(ref, ref, sems, base + k, to[device])
        yield
        s_up.wait_recv()
        r_up = pass_on(out_ref.at[at(3), lo], 3, "up")
        t_down = pass_on(out_ref.at[at(3)], 5, "twin")
        r_up.start()
        t_down.start()
        yield
        s_down.wait_recv()
        r_down = pass_on(out_ref.at[at(1), hi], 4, "down")
        t_up = pass_on(out_ref.at[at(1)], 6, "twin")
        r_down.start()
        t_up.start()
        yield
        r_up.wait_recv()
        t_lo = pass_on(out_ref.at[at(2), lo], 7, "twin")
        t_lo.start()
        yield
        r_down.wait_recv()
        t_hi = pass_on(out_ref.at[at(2), hi], 8, "twin")
        t_hi.start()
        pending += [s_up, s_down, s_twin, r_up, r_down, t_down, t_up, t_lo, t_hi]
        yield
        for copy in (s_twin, t_down, t_up, t_lo, t_hi):
            copy.wait_recv()
        mine.wait()


class SumTokens:
    peers = ("twin", "up", "down")
    n_sems = 10

    def __init__(self, rows, width):
        self.ins = [((8, rows, width), BF)]
        self.outs = [((rows, width), F32)]
        self.scratch = [
            pltpu.VMEM((4, rows, width), BF),
            pltpu.VMEM((3, rows, width), BF),
            pltpu.VMEM((rows, width), BF),
            pltpu.VMEM((3, rows, width), BF),
        ]
        self.rows = rows

    def run(self, ins, outs, scratch, sems, base, place, pending):
        y, c, _, _, to = place
        (p_ref,), (out_ref,) = ins, outs
        from_twin, pair, acc, near = scratch
        half = self.rows // 2
        cut = lambda v: (v.at[pl.ds(0, half)], v.at[pl.ds(half, half)])
        swaps = []
        for k, off in enumerate((2, 1, 3, 0)):
            at = lax.rem(y + off, 4) * 2
            copy = remote(p_ref.at[at + 1 - c], from_twin.at[k], sems, base + k, to["twin"])
            copy.start()
            swaps.append(copy)
        yield
        for k, off in enumerate((2, 1, 3)):
            swaps[k].wait_recv()
            pair[k] = add_low(p_ref[lax.rem(y + off, 4) * 2 + c], from_twin[k])
            if k == 0:
                far_plus = remote(
                    cut(pair.at[0])[0], cut(near.at[0])[0], sems, base + 4, to["up"]
                )
                far_minus = remote(
                    cut(pair.at[0])[1], cut(near.at[0])[1], sems, base + 5, to["down"]
                )
                far_plus.start()
                far_minus.start()
            elif k == 1:
                own_plus = remote(
                    cut(pair.at[1])[1], cut(near.at[1])[1], sems, base + 6, to["up"]
                )
                own_plus.start()
            else:
                own_minus = remote(
                    cut(pair.at[2])[0], cut(near.at[2])[0], sems, base + 7, to["down"]
                )
                own_minus.start()
        yield
        far_plus.wait_recv()
        cut(acc)[0][...] = add_low(cut(pair.at[1])[0][...], cut(near.at[0])[0][...])
        sum_plus = remote(cut(acc)[0], cut(near.at[1])[0], sems, base + 8, to["up"])
        sum_plus.start()
        yield
        far_minus.wait_recv()
        cut(acc)[1][...] = add_low(cut(pair.at[2])[1][...], cut(near.at[0])[1][...])
        sum_minus = remote(cut(acc)[1], cut(near.at[2])[1], sems, base + 9, to["down"])
        sum_minus.start()
        swaps[3].wait_recv()
        out_ref[...] = p_ref[y * 2 + c].astype(F32) + from_twin[3].astype(F32)
        pending += swaps + [far_plus, far_minus, own_plus, own_minus, sum_plus, sum_minus]
        yield
        for copy in (own_plus, own_minus, sum_plus, sum_minus):
            copy.wait_recv()
        out_ref[...] += near[1].astype(F32) + near[2].astype(F32)


def rows_or_columns(rows, width):
    if rows % 32 == 0:
        return lambda v: (v.at[pl.ds(0, rows // 2)], v.at[pl.ds(rows // 2, rows // 2)])
    return lambda v: (v.at[:, pl.ds(0, width // 2)], v.at[:, pl.ds(width // 2, width // 2)])


def firsts(v):
    return v.at[pl.ds(0, 2)], v.at[pl.ds(2, 2)]


class GatherWeights:
    peers = ("x+", "x-", "z+", "z-")
    n_sems = 17

    def __init__(self, rows, width):
        self.ins = [((rows, width), BF)]
        self.outs = [((4, 4, rows, width), BF)]
        self.scratch = []
        self.rows, self.width = rows, width

    def rings(self, out_ref, sems, base, place, pending):
        _, _, x, z, to = place
        first = self.width // 256 * 128
        a, b = pl.ds(0, first), pl.ds(first, self.width - first)
        every = pl.ds(0, self.rows)
        cut_a = rows_or_columns(self.rows, first)
        cut_b = rows_or_columns(self.rows, self.width - first)

        def along_x_first():
            yield from ring_gather(
                lambda j: out_ref.at[z, j, every, a], cut_a, x, to["x+"], to["x-"], sems, base, pending
            )
            yield from ring_gather(
                lambda j: out_ref.at[j, pl.ds(0, 4), every, a], firsts, z, to["z+"], to["z-"], sems, base + 4,
                pending,
            )

        def along_z_first():
            yield from ring_gather(
                lambda j: out_ref.at[j, x, every, b], cut_b, z, to["z+"], to["z-"], sems, base + 8, pending
            )
            yield from ring_gather(
                lambda j: out_ref.at[pl.ds(0, 4), j, every, b], firsts, x, to["x+"], to["x-"], sems,
                base + 12, pending,
            )

        yield from both(along_x_first(), along_z_first())

    def run(self, ins, outs, scratch, sems, base, place, pending):
        _, _, x, z, _ = place
        (x_ref,), (out_ref,) = ins, outs
        mine = pltpu.make_async_copy(x_ref, out_ref.at[z, x], sems.at[0, base + 16])
        mine.start()
        mine.wait()
        yield from self.rings(out_ref, sems, base, place, pending)


class SumWeights:
    peers = ("x+", "x-", "z+", "z-")
    n_sems = 24

    def __init__(self, rows, width):
        self.ins = [((4, 4, rows, width), BF)]
        self.outs = [((rows, width), BF)]
        self.rows, self.width = rows, width
        first = width // 256 * 128
        self.widths = (first, width - first)
        self.scratch = []
        for w in self.widths:
            self.scratch += [
                pltpu.VMEM((4, rows, w), BF),
                pltpu.VMEM((3, 4, rows, w), BF),
                pltpu.VMEM((4, rows, w), BF),
                pltpu.VMEM((rows, w), BF),
                pltpu.VMEM((3, rows, w), BF),
            ]

    def run(self, ins, outs, scratch, sems, base, place, pending):
        _, _, x, z, to = place
        (p_ref,), (out_ref,) = ins, outs
        every = pl.ds(0, self.rows)

        def one(order, bufs, base):
            acc, near, total, acc_two, near_two = bufs
            width = self.widths[order]
            columns = pl.ds(order * self.widths[0], width)
            cut = rows_or_columns(self.rows, width)
            four = pl.ds(0, 4)
            if order == 0:
                block = lambda j: p_ref.at[four, j, every, columns]
                i, k, far, close = x, z, ("x+", "x-"), ("z+", "z-")
            else:
                block = lambda j: p_ref.at[j, four, every, columns]
                i, k, far, close = z, x, ("z+", "z-"), ("x+", "x-")
            yield from ring_scatter(
                block, firsts, i, to[far[0]], to[far[1]], acc, near, sems, base, pending
            )
            total[...] = (
                block(i)[...].astype(F32) + near[1].astype(F32) + near[2].astype(F32)
            ).astype(BF)
            yield from ring_scatter(
                lambda j: total.at[j], cut, k, to[close[0]], to[close[1]], acc_two, near_two, sems,
                base + 6, pending,
            )
            out_ref[every, columns] = (
                total[k].astype(F32) + near_two[1].astype(F32) + near_two[2].astype(F32)
            ).astype(BF)

        yield from both(one(0, scratch[:5], base), one(1, scratch[5:], base + 12))


class Swap:
    peers = ("twin", "up", "down", "across", "up_twin", "down_twin", "across_twin")
    n_sems = 8
    steps = ((0, 1), (1, 0), (3, 0), (2, 0), (1, 1), (3, 1), (2, 1))

    def __init__(self, rows, width):
        self.ins = [((8, rows, width), BF)]
        self.outs = [((8, rows, width), BF)]
        self.scratch = []

    def send(self, x_ref, out_ref, sems, base, place):
        y, c, _, _, to = place
        me = y * 2 + c
        copies = [pltpu.make_async_copy(x_ref.at[me], out_ref.at[me], sems.at[0, base + 7])]
        for k, (name, (up, other)) in enumerate(zip(self.peers, self.steps)):
            at = lax.rem(y + up, 4) * 2 + (1 - c if other else c)
            copies.append(remote(x_ref.at[at], out_ref.at[me], sems, base + k, to[name]))
        for copy in copies:
            copy.start()
        return copies

    def run(self, ins, outs, scratch, sems, base, place, pending):
        copies = self.send(ins[0], outs[0], sems, base, place)
        yield
        copies[0].wait()
        for copy in copies[1:]:
            copy.wait_recv()
        pending += copies[1:]


class SwapThenGather:
    peers = Swap.peers + GatherWeights.peers

    def __init__(self, rows, width):
        self.swap = Swap(rows, width)
        self.gather = GatherWeights(8 * rows, width)
        self.ins = self.swap.ins
        self.outs = self.gather.outs
        self.scratch = [pltpu.VMEM((8, rows, width), BF)]
        self.rows, self.width = rows, width
        self.n_sems = 8 + 8 + self.gather.n_sems

    def run(self, ins, outs, scratch, sems, base, place, pending):
        _, _, x, z, _ = place
        (out_ref,), (landed,) = outs, scratch
        yield from self.swap.run(ins, (landed,), (), sems, base, place, pending)
        for k in range(8):
            out_ref[z, x, k * self.rows : (k + 1) * self.rows] = landed[k]
        yield from self.gather.rings(out_ref, sems, base + 16, place, pending)


class SwapThenSum:
    peers = Swap.peers + SumWeights.peers

    def __init__(self, rows, width):
        self.swap = Swap(rows, width)
        self.sum = SumWeights(rows, width)
        self.ins = self.swap.ins
        self.outs = self.sum.outs
        self.scratch = [
            pltpu.VMEM((8, rows, width), BF),
            pltpu.VMEM((4, 4, rows, width), BF),
        ] + self.sum.scratch
        self.n_sems = 8 + self.sum.n_sems

    def run(self, ins, outs, scratch, sems, base, place, pending):
        landed, spread = scratch[:2]
        yield from self.swap.run(ins, (landed,), (), sems, base, place, pending)
        total = jnp.sum(landed[...].astype(F32), axis=0).astype(BF)
        spread[...] = jnp.broadcast_to(total[None, None], spread.shape)
        yield from self.sum.run((spread,), outs, scratch[2:], sems, base + 8, place, pending)


def both(*parts):
    parts = list(parts)
    while parts:
        for part in list(parts):
            try:
                next(part)
            except StopIteration:
                parts.remove(part)
        yield


def in_order(parts, order):
    for letter in order:
        next(parts["abcdef".index(letter)], None)
    for _ in both(*parts):
        pass


def size(shape, dtype):
    return math.prod(shape) * jnp.dtype(dtype).itemsize


def comm_kernel(parts, order, *refs):
    sems = refs[-1]
    n_in = sum(len(p.ins) for p in parts)
    n_out = sum(len(p.outs) for p in parts)
    ins, outs, scratch = list(refs[:n_in]), list(refs[n_in : n_in + n_out]), list(refs[n_in + n_out : -1])
    place = places()
    names = []
    for p in parts:
        names += [n for n in p.peers if n not in names]
    barrier = pltpu.get_barrier_semaphore()
    for name in names:
        pl.semaphore_signal(
            barrier, inc=1, device_id=place[4][name], device_id_type=pl.DeviceIdType.MESH
        )
    pl.semaphore_wait(barrier, len(names))
    base, running, pending = 0, [], []
    for p in parts:
        taken = []
        for refs_of, count in ((ins, len(p.ins)), (outs, len(p.outs)), (scratch, len(p.scratch))):
            taken.append([refs_of.pop(0) for _ in range(count)])
        running.append(p.run(*taken, sems, base, place, pending))
        base += p.n_sems
    in_order(running, order)
    for copy in pending:
        copy.wait_send()


def comm(collective_id, order, *pairs):
    parts = [p for p, _ in pairs]
    operands = [x.reshape(spec[0]) for p, xs in pairs for x, spec in zip(xs, p.ins)]
    spaces = [spec[2] if len(spec) > 2 else pltpu.VMEM for p in parts for spec in p.ins]
    outs = [o for p in parts for o in p.outs]
    held = sum(size(*spec[:2]) for p in parts for spec in p.ins + p.outs)
    held += sum(size(s.shape, s.dtype) for p in parts for s in p.scratch)
    sent = sum(math.prod(shape) for shape, _ in outs) * 2
    return pl.pallas_call(
        functools.partial(comm_kernel, parts, order),
        out_shape=[jax.ShapeDtypeStruct(*o) for o in outs],
        in_specs=[pl.BlockSpec(memory_space=space) for space in spaces],
        out_specs=[pl.BlockSpec(memory_space=pltpu.VMEM)] * len(outs),
        scratch_shapes=[s for p in parts for s in p.scratch]
        + [pltpu.SemaphoreType.DMA((2, sum(p.n_sems for p in parts)))],
        compiler_params=pltpu.CompilerParams(
            collective_id=collective_id, has_side_effects=True, vmem_limit_bytes=held + (10 << 20)
        ),
        cost_estimate=pl.CostEstimate(flops=0, bytes_accessed=20 * sent, transcendentals=0),
    )(*operands)


ROWS = 256


def qkv_kernel(u_ref, w_ref, gain_ref, shift_ref, bias_ref, c_ref, a_ref, b_ref, h_ref, out_ref):
    h = (u_ref[...].astype(F32) * gain_ref[...] + shift_ref[...]).astype(BF)
    h_ref[...] = h
    mixed = dot_nn(h, w_ref[:, 0:768]) + bias_ref[...]
    for j in range(6):
        part = mixed[:, j * 128 : (j + 1) * 128]
        if j % 3 < 2:
            part = rotate(part, c_ref[...], a_ref[...], b_ref[...])
        out_ref[:, j * 128 : (j + 1) * 128] = part.astype(BF)


def rowwise(width):
    return pl.BlockSpec((ROWS, width), lambda i: (i, 0))


def fixed(*shape):
    return pl.BlockSpec(shape, lambda i: (0,) * len(shape))


def qkv_call(u, w, gain, shift, bias, tables):
    return pl.pallas_call(
        qkv_kernel,
        out_shape=(
            jax.ShapeDtypeStruct((HALF, D), BF),
            jax.ShapeDtypeStruct((HALF, 768), BF),
        ),
        grid=(HALF // ROWS,),
        in_specs=[rowwise(D), fixed(D, 896), fixed(1, D), fixed(1, D), fixed(1, 768)]
        + [rowwise(128)] * 3,
        out_specs=(rowwise(D), rowwise(768)),
        compiler_params=pltpu.CompilerParams(vmem_limit_bytes=40 << 20),
        cost_estimate=pl.CostEstimate(
            flops=2 * HALF * D * 768, bytes_accessed=14 << 20, transcendentals=0
        ),
    )(u, w, gain, shift, bias, *tables)


BLOCK = 512
Q, K, V = slice(0, 128), slice(128, 256), slice(256, 384)


def only(x, h):
    lane = lax.broadcasted_iota(jnp.int32, (1, 128), 1)
    return jnp.where((lane >= h * HEAD) & (lane < (h + 1) * HEAD), x, jnp.zeros_like(x))


def rows_of(k):
    return slice(k * BLOCK, (k + 1) * BLOCK)


def allowed_mask(first_len, key_half, kb, query_half, qb, diagonal):
    key = lax.broadcasted_iota(jnp.int32, (BLOCK, BLOCK), 0) + kb * BLOCK
    query = lax.broadcasted_iota(jnp.int32, (BLOCK, BLOCK), 1) + qb * BLOCK
    allowed = None
    if diagonal and kb == qb:
        allowed = key <= query
    if kb == 0:
        same = (key + key_half * HALF >= first_len) | (query + query_half * HALF < first_len)
        allowed = same if allowed is None else allowed & same
    return allowed


def lanes(at, width):
    return pl.ds(pl.multiple_of(at * width, 128), width)


class Attend:
    peers = ("pair",)
    n_sems = 6

    def __init__(self):
        self.ins = [((1, 1), jnp.int32, pltpu.SMEM), ((HALF, 768), BF)]
        self.outs = [
            ((HALF, 256), BF),
            ((2, 128, HALF), F32),
            ((2, 8, HALF), F32),
            ((2, HALF, 384), BF),
        ]
        self.scratch = [pltpu.VMEM((2, 8, HALF), F32), pltpu.VMEM((2, HALF, 128), BF)]

    def run(self, ins, outs, scratch, sems, base, place, pending):
        len_ref, qkv_ref = ins
        o_ref, acc_ref, top_ref, x_ref = outs
        total_ref, half_ref = scratch
        pair = place[4]["pair"]
        xl = lax.axis_index("xl")
        first_len = len_ref[0, 0]
        sent = []
        for b in range(2):
            copy = remote(
                qkv_ref.at[rows_of(b), lanes(1 - xl, 384)], x_ref.at[xl, rows_of(b)], sems, base + b, pair
            )
            copy.start()
            sent.append(copy)
        kept = pltpu.make_async_copy(qkv_ref.at[:, lanes(xl, 384)], x_ref.at[xl], sems.at[0, base + 2])
        kept.start()
        kept.wait()
        yield

        def block(query_half, key_half, qb, h, state, diagonal):
            qs = rows_of(qb)
            qh = only(x_ref[query_half, qs, Q] * jnp.asarray(HEAD**-0.5, BF), h)
            top, total, acc = state
            for kb in range(qb + 1 if diagonal else 2):
                ks = rows_of(kb)
                scores = dot_nt(x_ref[key_half, ks, K], qh)
                allowed = allowed_mask(first_len, key_half, kb, query_half, qb, diagonal)
                if allowed is not None:
                    scores = jnp.where(allowed, scores, MASKED)
                new_top = jnp.maximum(top, jnp.max(scores, axis=0, keepdims=True))
                weights = jnp.exp(scores - new_top)
                if allowed is not None:
                    weights = jnp.where(allowed, weights, 0.0)
                shrink = jnp.exp(top - new_top)
                total = total * shrink + jnp.sum(weights, axis=0, keepdims=True)
                part = dot_tn(only(x_ref[key_half, ks, V], h), weights.astype(BF))
                acc = acc * shrink + part[h * HEAD : (h + 1) * HEAD]
                top = new_top
            top_ref[query_half, h : h + 1, qs] = top
            total_ref[query_half, h : h + 1, qs] = total
            acc_ref[query_half, h * HEAD : (h + 1) * HEAD, qs] = acc

        def diagonal(half):
            for qb in range(2):
                for h in range(2):
                    start = (
                        jnp.full((1, BLOCK), MASKED, F32),
                        jnp.zeros((1, BLOCK), F32),
                        jnp.zeros((HEAD, BLOCK), F32),
                    )
                    block(half, half, qb, h, start, True)

        def finish(half):
            for qb in range(2):
                qs = rows_of(qb)
                for h in range(2):
                    hs = slice(h * HEAD, (h + 1) * HEAD)
                    total = total_ref[half, h : h + 1, qs]
                    acc_ref[half, hs, qs] = acc_ref[half, hs, qs] / total
                    top_ref[half, h : h + 1, qs] = top_ref[half, h : h + 1, qs] + jnp.log(total)
                half_ref[half, qs, :] = acc_ref[half, :, qs].T.astype(BF)

        diagonal(xl)
        yield
        for copy in sent:
            copy.wait_recv()
        diagonal(1 - xl)
        yield
        for qb in range(2):
            for h in range(2):
                qs = rows_of(qb)
                state = (
                    top_ref[1, h : h + 1, qs],
                    total_ref[1, h : h + 1, qs],
                    acc_ref[1, h * HEAD : (h + 1) * HEAD, qs],
                )
                block(1, 0, qb, h, state, False)
            yield
        finish(1 - xl)
        back = remote(half_ref.at[1 - xl], o_ref.at[:, lanes(xl, 128)], sems, base + 3, pair)
        back.start()
        finish(xl)
        mine = pltpu.make_async_copy(half_ref.at[xl], o_ref.at[:, lanes(xl, 128)], sems.at[0, base + 4])
        mine.start()
        pending += sent + [back]
        yield
        mine.wait()
        back.wait_recv()


class AttendBack:
    peers = ("pair",)
    n_sems = 6

    def __init__(self):
        self.ins = [
            ((1, 1), jnp.int32, pltpu.SMEM),
            ((2, HALF, 384), BF),
            ((HALF, 256), BF),
            ((2, 128, HALF), F32),
            ((2, 8, HALF), F32),
        ] + [((2, HALF, 128), F32)] * 3
        self.outs = [((HALF, 768), BF)]
        self.scratch = [
            pltpu.VMEM((2, HALF, 128), BF),
            pltpu.VMEM((2, 128, HALF), F32),
            pltpu.VMEM((2, HALF, 128), F32),
            pltpu.VMEM((2, HALF, 128), F32),
            pltpu.VMEM((2, HALF, 384), BF),
        ]

    def run(self, ins, outs, scratch, sems, base, place, pending):
        len_ref, x_ref, own_ref, ot_ref, lse_ref, c_ref, a_ref, b_ref = ins
        (out_ref,) = outs
        do_ref, dqt_ref, dk_ref, dv_ref, half_ref = scratch
        pair = place[4]["pair"]
        xl = lax.axis_index("xl")
        first_len = len_ref[0, 0]
        sent = remote(own_ref.at[:, lanes(1 - xl, 128)], do_ref.at[xl], sems, base, pair)
        sent.start()
        kept = pltpu.make_async_copy(own_ref.at[:, lanes(xl, 128)], do_ref.at[xl], sems.at[0, base + 1])
        kept.start()
        kept.wait()
        yield

        def block(query_half, key_half, qb, h, diagonal):
            qs = rows_of(qb)
            hs = slice(h * HEAD, (h + 1) * HEAD)
            do = do_ref[query_half, qs, :]
            qh = only(x_ref[query_half, qs, Q] * jnp.asarray(HEAD**-0.5, BF), h)
            doh = only(do, h)
            delta = jnp.sum(
                doh.astype(F32).T[hs] * ot_ref[query_half, hs, qs], axis=0, keepdims=True
            )
            lse = lse_ref[query_half, h : h + 1, qs]
            for kb in range(qb + 1 if diagonal else 2):
                ks = rows_of(kb)
                k = x_ref[key_half, ks, K]
                scores = dot_nt(k, qh)
                probs = jnp.exp(scores - lse)
                allowed = allowed_mask(first_len, key_half, kb, query_half, qb, diagonal)
                if allowed is not None:
                    probs = jnp.where(allowed, probs, 0.0)
                pulled = dot_nt(x_ref[key_half, ks, V], doh)
                ds = (probs * (pulled - delta)).astype(BF)
                dv = dot_nn(probs.astype(BF), doh)
                dk = dot_nn(ds, qh)
                dq = dot_tn(only(k, h), ds)[hs]
                if diagonal and h == 0 and qb == kb:
                    dv_ref[key_half, ks, :] = dv
                    dk_ref[key_half, ks, :] = dk
                else:
                    dv_ref[key_half, ks, :] += dv
                    dk_ref[key_half, ks, :] += dk
                if diagonal and kb == 0:
                    dqt_ref[query_half, hs, qs] = dq
                else:
                    dqt_ref[query_half, hs, qs] += dq

        def finish(half):
            for b in range(2):
                bs = rows_of(b)
                c, below, above = c_ref[half, bs, :], -a_ref[half, bs, :], -b_ref[half, bs, :]
                dq = dqt_ref[half, :, bs].T * HEAD**-0.5
                half_ref[half, bs, Q] = rotate(dq, c, below, above).astype(BF)
                half_ref[half, bs, K] = rotate(dk_ref[half, bs, :], c, below, above).astype(BF)
                half_ref[half, bs, V] = dv_ref[half, bs, :].astype(BF)

        for qb in range(2):
            for h in range(2):
                block(xl, xl, qb, h, True)
        yield
        sent.wait_recv()
        for qb in range(2):
            for h in range(2):
                block(1 - xl, 1 - xl, qb, h, True)
        yield
        for qb in range(2):
            for h in range(2):
                block(1, 0, qb, h, False)
            yield
        finish(1 - xl)
        back = remote(half_ref.at[1 - xl], out_ref.at[:, lanes(xl, 384)], sems, base + 2, pair)
        back.start()
        finish(xl)
        mine = pltpu.make_async_copy(half_ref.at[xl], out_ref.at[:, lanes(xl, 384)], sems.at[0, base + 3])
        mine.start()
        pending += [sent, back]
        yield
        mine.wait()
        back.wait_recv()


def feed_kernel(h_ref, dy_ref, gate_ref, up_ref, down_ref, hid_ref, dg_ref, du_ref, dh_ref, y_ref):
    gate, up = dot_nn(h_ref[...], gate_ref[...]), dot_nn(h_ref[...], up_ref[...])
    sigmoid = jax.nn.sigmoid(gate)
    activated = gate * sigmoid
    hidden = (activated * up).astype(BF)
    hid_ref[...] = hidden
    d_hidden = dot_nt(dy_ref[...], down_ref[...])
    d_gate = (d_hidden * up * sigmoid * (1.0 + gate * (1.0 - sigmoid))).astype(BF)
    d_up = (d_hidden * activated).astype(BF)
    dg_ref[...] = d_gate
    du_ref[...] = d_up
    dh_ref[...] = (dot_nt(d_gate, gate_ref[...]) + dot_nt(d_up, up_ref[...])).astype(BF)
    y_ref[...] = dot_nn(hidden, down_ref[...]).astype(BF)


def feed_call(h, dy, w_gate, w_up, w_down):
    return pl.pallas_call(
        feed_kernel,
        out_shape=(
            jax.ShapeDtypeStruct((HALF, 768), BF),
            jax.ShapeDtypeStruct((HALF, 768), BF),
            jax.ShapeDtypeStruct((HALF, 768), BF),
            jax.ShapeDtypeStruct((HALF, D), BF),
            jax.ShapeDtypeStruct((HALF, D), BF),
        ),
        grid=(HALF // ROWS,),
        in_specs=[rowwise(D), rowwise(D), fixed(D, 768), fixed(D, 768), fixed(768, D)],
        out_specs=(rowwise(768), rowwise(768), rowwise(768), rowwise(D), rowwise(D)),
        compiler_params=pltpu.CompilerParams(vmem_limit_bytes=56 << 20),
        cost_estimate=pl.CostEstimate(
            flops=6 * 2 * HALF * D * 768, bytes_accessed=30 << 20, transcendentals=HALF * 768
        ),
    )(h, dy, w_gate, w_up, w_down)


def weight_grad_kernel(n, a_ref, *refs):
    for b_ref, out_ref in zip(refs[:n], refs[n:]):
        out_ref[...] = dot_tn(a_ref[...], b_ref[...]).astype(BF)


def weight_grad(a, step, *others):
    rows = a.shape[1]
    return pl.pallas_call(
        functools.partial(weight_grad_kernel, len(others)),
        out_shape=[jax.ShapeDtypeStruct((rows, b.shape[1]), BF) for b in others],
        grid=(rows // step,),
        in_specs=[pl.BlockSpec((HALF, step), lambda i: (0, i))] + [fixed(*b.shape) for b in others],
        out_specs=[pl.BlockSpec((step, b.shape[1]), lambda i: (i, 0)) for b in others],
        compiler_params=pltpu.CompilerParams(vmem_limit_bytes=40 << 20),
        cost_estimate=pl.CostEstimate(
            flops=2 * HALF * rows * sum(b.shape[1] for b in others),
            bytes_accessed=12 << 20,
            transcendentals=0,
        ),
    )(a, *others)


def last_kernel(dx_ref, u_ref, w_ref, dh_ref, sums_ref, bias_ref):
    dh = dot_nt(dx_ref[...], w_ref[:, 0:768])
    dh_ref[...] = dh.astype(BF)

    @pl.when(pl.program_id(0) == 0)
    def _():
        sums_ref[...] = jnp.zeros_like(sums_ref)
        bias_ref[...] = jnp.zeros_like(bias_ref)

    sums_ref[0:1] += jnp.sum(dh * u_ref[...].astype(F32), axis=0, keepdims=True)
    sums_ref[1:2] += jnp.sum(dh, axis=0, keepdims=True)
    bias_ref[0:1] += jnp.sum(dx_ref[...].astype(F32), axis=0, keepdims=True)


def last_call(dx, u, w):
    return pl.pallas_call(
        last_kernel,
        out_shape=(
            jax.ShapeDtypeStruct((HALF, D), BF),
            jax.ShapeDtypeStruct((8, D), F32),
            jax.ShapeDtypeStruct((8, 768), F32),
        ),
        grid=(HALF // ROWS,),
        in_specs=[rowwise(768), rowwise(D), fixed(D, 896)],
        out_specs=(rowwise(D), fixed(8, D), fixed(8, 768)),
        compiler_params=pltpu.CompilerParams(vmem_limit_bytes=40 << 20),
        cost_estimate=pl.CostEstimate(
            flops=2 * HALF * D * 768, bytes_accessed=14 << 20, transcendentals=0
        ),
    )(dx, u, w)


TO_HEADS = [(f * 16 + ctx, ctx * 8 + f) for f in range(8) for ctx in range(16)]
TO_OWNER = [(b, a) for a, b in TO_HEADS]


def hidden_columns(weight):
    split = weight.astype(BF).reshape(16, 16, 8, 44).transpose(2, 0, 1, 3)
    return jnp.pad(split, ((0, 0), (0, 0), (0, 0), (0, 4))).reshape(8, 16, 768)


def hidden_columns_back(grad):
    return grad.reshape(8, 16, 16, 48)[..., :44].transpose(1, 2, 0, 3).reshape(16, FF)


def local(
    hidden_in, out_grad, positions, documents,
    qkv_weight, qkv_first, qkv_second,
    out_weight, out_first, out_second,
    gate_weight, gate_first, gate_second,
    up_weight, up_first, up_second,
    down_weight, down_first, down_second,
    small_params, small_first, small_second,
):
    xh, xl, z = lax.axis_index("xh"), lax.axis_index("xl"), lax.axis_index("z")
    yc = lax.axis_index("y") * 2 + lax.axis_index("core")
    place = (z * 2 + xh) * 2 + xl

    first_here = jnp.sum(1 - documents)
    start_here = positions[0, 0]
    marks = jnp.stack([first_here, start_here // 64, start_here % 64]).astype(BF)
    tile = jnp.concatenate(
        [small_params.astype(BF), jnp.pad(marks, (0, 13))[None]], axis=0
    )
    tile = jnp.pad(tile, ((0, 8), (0, 112)))
    qkv_piece = jnp.concatenate(
        [
            qkv_weight.astype(BF).reshape(16, 3, 8, 2, 128).transpose(2, 0, 3, 1, 4).reshape(8, 16, 768),
            jnp.broadcast_to(tile[None], (8, 16, 128)),
        ],
        axis=2,
    )
    rows = hidden_in.reshape(128, D).astype(F32)
    outer = out_grad.reshape(128, D)
    mean = jnp.mean(rows, axis=-1, keepdims=True)
    centred = rows - mean
    scale_one = lax.rsqrt(jnp.mean(centred * centred, axis=-1, keepdims=True) + NORM_EPS)
    unit_one = centred * scale_one
    gu_piece = jnp.concatenate([hidden_columns(gate_weight), hidden_columns(up_weight)], axis=2)
    w_all, u_all, gu_mine = comm(
        0,
        "aabcaaabbaabbabc",
        (SwapThenGather(16, 896), (qkv_piece,)),
        (GatherTokens(128, D), (unit_one.astype(BF),)),
        (Swap(16, 1536), (gu_piece,)),
    )
    gu_mine = gu_mine.reshape(128, 1536)
    w_gate = lax.all_gather(gu_mine[:, :768], ZX, axis=0, tiled=True)
    u_all = u_all.reshape(HALF, D)
    w_qkv = w_all.reshape(D, 896)

    tiles = w_qkv[:, 768:784].reshape(128, 16, 16)
    params = tiles[:, :7].transpose(1, 0, 2).reshape(7, D).astype(F32)
    marks = lax.dynamic_index_in_dim(tiles[:, 7, :3], (z * 2 + xh) * 16, keepdims=False)
    marks = marks.astype(jnp.int32)
    first_len = marks[0]
    step = jnp.arange(SEQ)
    tables = rotary_tables(
        jnp.where(step < first_len, marks[1] * 64 + marks[2] + step, 4095 + step)
    )
    first_len = first_len.reshape(1, 1)
    half_tables = [lax.dynamic_slice_in_dim(t, xl * HALF, HALF, axis=0) for t in tables]
    bias = lax.dynamic_slice_in_dim(params[2:5], yc * 256, 256, axis=1)
    bias = bias.reshape(3, 2, 128).transpose(1, 0, 2).reshape(1, 768)

    h1, qkv = qkv_call(u_all, w_qkv, params[0:1], params[1:2], bias, half_tables)
    out_rows = lax.ppermute(out_weight.astype(BF), AXES, TO_HEADS)
    o, attended_t, lse, heads, w_out, dy = comm(
        1,
        "acaccabccabbbacbbaba",
        (Attend(), (first_len, qkv)),
        (GatherWeights(16, D), (out_rows,)),
        (GatherTokens(128, D), (outer,)),
    )
    w_out, dy = w_out.reshape(256, D), dy.reshape(HALF, D)
    branch_part = dot_nn(o, w_out).astype(BF)
    branch, w_up = comm(
        2,
        "ababbbaabbab",
        (SumTokens(128, D), (branch_part,)),
        (GatherWeights(128, 768), (gu_mine[:, 768:],)),
    )
    middle = rows + branch
    normed_two, unit_two, scale_two = norm_forward(middle, params[5], params[6])
    down_piece = jnp.pad(down_weight.astype(BF), ((0, 4), (0, 0)))
    h2, w_down = comm(
        3,
        "abbbbaabbaaab",
        (GatherTokens(128, D), (normed_two.astype(BF),)),
        (GatherWeights(48, D), (down_piece,)),
    )
    h2 = h2.reshape(HALF, D)
    hidden, d_gate_low, d_up_low, dh2_part, y_part = feed_call(
        h2, dy, w_gate, w_up.reshape(D, 768), w_down.reshape(768, D)
    )

    (d_down,) = weight_grad(hidden, 256, dy)
    d_gate, d_up = weight_grad(h2, 512, d_gate_low, d_up_low)
    g_up = lax.psum_scatter(d_up, ZX, scatter_dimension=0, tiled=True)
    d_normed_two, g_down = comm(
        4, "ababbaabbbab", (SumTokens(128, D), (dh2_part,)), (SumWeights(48, D), (d_down,))
    )
    d_middle_part, d_gain_two, d_shift_two = norm_backward(
        d_normed_two, unit_two, scale_two, params[5]
    )
    d_middle = outer.astype(F32) + d_middle_part
    dx2, g_gate = comm(
        5, "abbbaabbbaaab", (GatherTokens(128, D), (d_middle.astype(BF),)), (SumWeights(128, 768), (d_gate,))
    )
    dx2 = dx2.reshape(HALF, D)
    do = dot_nt(dx2, w_out).astype(BF)
    d_qkv_low, branch_two = comm(
        7,
        "abaaaaabbbba",
        (
            AttendBack(),
            (first_len, heads, do, attended_t, lse, *[t.reshape(2, HALF, 128) for t in tables]),
        ),
        (SumTokens(128, D), (y_part,)),
    )
    block_out = (middle + branch_two).reshape(1, 128, D).astype(BF)
    d_out = dot_tn(o, dx2).astype(BF)
    dh1_part, sums, d_bias = last_call(d_qkv_low, u_all, w_qkv)
    (d_qkv,) = weight_grad(h1, 512, d_qkv_low)
    d_bias = d_bias[0].reshape(2, 3, 128).transpose(1, 0, 2).reshape(3, 256)
    d_small = jnp.concatenate(
        [
            sums[0:2],
            lax.dynamic_update_slice_in_dim(jnp.zeros((3, D), F32), d_bias, yc * 256, axis=1),
            d_gain_two[None],
            d_shift_two[None],
            jnp.zeros((9, D), F32),
        ],
        axis=0,
    )
    small_piece = d_small.astype(BF).reshape(16, 16, 8, 16).transpose(2, 0, 1, 3).reshape(8, 16, 256)
    small_piece = jnp.pad(small_piece, ((0, 0), (0, 0), (0, 256)))
    d_normed, g_qkv, g_out, g_small = comm(
        6,
        "abcdabbccdaabcdddbbccddabcd",
        (SumTokens(128, D), (dh1_part,)),
        (SumWeights(128, 768), (d_qkv,)),
        (SumWeights(16, D), (d_out,)),
        (SwapThenSum(16, 512), (small_piece,)),
    )
    d_rows_part = norm_backward(d_normed, unit_one, scale_one, params[0])[0]
    input_grad = (d_middle + d_rows_part).reshape(1, 128, D)

    g_out = lax.ppermute(g_out, AXES, TO_OWNER).astype(F32)
    (back,) = comm(8, "", (Swap(16, 2304), (jnp.concatenate([g_qkv, g_gate, g_up], axis=1),)))
    g_qkv = back[..., :768].reshape(8, 16, 2, 3, 128).transpose(1, 3, 0, 2, 4).reshape(16, 3 * D)
    g_gate = hidden_columns_back(back[..., 768:1536])
    g_up = hidden_columns_back(back[..., 1536:])
    g_small = lax.dynamic_index_in_dim(
        g_small[:, :256].reshape(16, 16, 16), place, axis=1, keepdims=False
    )[:7].astype(F32)

    updates = (
        adamw(qkv_weight, qkv_first, qkv_second, g_qkv.astype(F32), D ** (-0.5), 0.1),
        adamw(out_weight, out_first, out_second, g_out, (D // 16) ** (-0.5), 0.1),
        adamw(gate_weight, gate_first, gate_second, g_gate.astype(F32), D ** (-0.5), 0.1),
        adamw(up_weight, up_first, up_second, g_up.astype(F32), D ** (-0.5), 0.1),
        adamw(down_weight, down_first, down_second, g_down[:44].astype(F32), FF ** (-0.5), 0.1),
        adamw(small_params, small_first, small_second, g_small, 2.0, 0.0),
    )
    return (block_out, input_grad, *[x for u in updates for x in u])


def solution(mesh):
    fine = Mesh(mesh.devices.reshape(4, 2, 2, 4, 2), AXES)
    tokens = P(("z", "xh"), ("xl", "y", "core"), None)
    marks = P(("z", "xh"), ("xl", "y", "core"))
    rows = P(AXES, None)
    small = P(None, AXES)
    in_specs = (tokens, tokens, marks, marks) + (rows,) * 15 + (small,) * 3
    out_specs = (tokens, tokens) + (rows,) * 15 + (small,) * 3
    return jax.shard_map(local, mesh=fine, in_specs=in_specs, out_specs=out_specs, check_vma=False)
```

time: 2250 us -> 479 us (0.21)
  waiting for transfers between devices: 1530 us -> 0.04 us
  Pallas kernels: 0 us -> 339 us
  matrix products: 254 us -> 3.81 us
  local copies, waits for them, and re-layouts: 289 us -> 50.8 us
  blocking collectives: 74.2 us -> 0 us
  other arithmetic: 71.8 us -> 41.8 us
    unnamed x12 -> x2, waiting for transfers between devices: 1150 us -> 0.03 us
    pallas_call x0 -> x15, Pallas kernels: none -> 339 us  [the longest x9 282 us: comm(): pl.pallas_call(functools.partial(comm_kernel, parts, order), out_shape=[j...]
    all_gather x3 -> x1, waiting for transfers between devices: 282 us -> 0.01 us  [local(): w_gate = lax.all_gather(gu_mine[:, :768], ZX, axis=0, tiled=True)]
    dot_general x39 -> x3, matrix products: 254 us -> 3.81 us  [the longest x1 1.29 us: dot_nt(): lax.dot_general(a, b, (((1,), (1,)), ((), ())), preferred_element_type=F32)]
    unnamed x114 -> x148, local copies, waits for them, and re-layouts: 169 us -> 32.2 us
    reduce_scatter x1, waiting for transfers between devices: 101 us -> 0.01 us  [local(): g_up = lax.psum_scatter(d_up, ZX, scatter_dimension=0, tiled=True)]
    convert_element_type x12 -> x7, local copies, waits for them, and re-layouts: 46.1 us -> 4.62 us  [the longest x2 1.95 us: local(): g_gate.astype(F32)]
    all_gather x1 -> x0, blocking collectives: 37.4 us -> none  [local(): lax.all_gather(small_low, ('fsdp', 'ctx'), axis=1, tiled=True)]
  transfers between devices with their start and end apart: 8 -> 4, of which waited for: 8 -> 0; matrix products, arithmetic and copies ran while one was open for 8% -> 8% of each run, Pallas kernels for 0% -> 48%
where the time goes in v1:
time: 479 us; the launch traced here: 470 us
  Pallas kernels  339 us (71%)
  local copies, waits for them, and re-layouts  50.8 us (11%)
  other arithmetic  41.8 us (9%)
  between operations  20.4 us (4%)
  starting transfers between devices  14.4 us (3%)
    pallas_call x9, Pallas kernels, comm(): pl.pallas_call(functools.partial(comm_kernel, parts, order), out_shape=[j...  282 us
    unnamed x148, local copies, waits for them, and re-layouts  32.2 us
    pallas_call x1, Pallas kernels, feed_call(): pl.pallas_call(feed_kernel, out_shape=(jax.ShapeDtypeStruct((HALF, 768),...  28 us
    pallas_call x3, Pallas kernels, weight_grad(): pl.pallas_call(functools.partial(weight_grad_kernel, len(others)), out_sh...  16.1 us
    sub x6, other arithmetic, adamw(): weight - rate * (mean_hat / (jnp.sqrt(square_hat) + ADAM_EPS) + decay * w...  10.5 us
  transfers between devices with their start and end apart: 4, of which 0 were waited for; matrix products, arithmetic and copies ran while one was open for 8% of the time, Pallas kernels for 48%

profile of v1, /device:TPU:25, one launch (start us, length us, event | category | flops | bytes accessed | tf_op | source)
XLA Modules:
  0.0 469.8 jit_solution(16107520045147659366)
XLA Ops:
  9.9 1.3 subtract_reduce_fusion
  12.6 1.0 convert_element_type.137
  14.0 1.2 convert_reduce_fusion
  15.3 1.3 fusion.14
  17.5 1.5 reshape.300
  19.7 1.5 reshape.302
  22.1 37.0 %shard_map.383 = (bf16[4,4,128,896]{3,2,1,0:T(8,128)(2,1)S(1)}, bf16[8,128,2048]{2,1,0:T(8,128)(2,1)S(1)}, bf16[8,16,1536]{2,1,0:T(8,128)(2,1)S(1)}) custom-call(bf16[8,16,896]{2,1,0:T(8,128)(2,1)S(1)} %pad_maximum_fusion.2.refs_0_, bf16[128,2048]{1,0:T(8,128)(2,1)S(1)} %fusion.8.refs_1_, bf16[8,16,1536]{2,1,0:T(8,128)(2,1)S(1)} %pad_maximum_fusion.1.refs_2_), custom_call_target="tpu_custom_call" | custom-call | bytes 165150720 | tf_op jit(solution)/shard_map/pallas_call | solution.py:533
  59.1 1.8 copy-done.19
  60.9 2.0 copy-done.24
  64.3 7.5 %collective-permute-start = (bf16[16,2048]{1,0:T(8,128)(2,1)}, bf16[16,2048]{1,0:T(8,128)(2,1)S(1)}, u32[]{:S(2)}, u32[]{:S(2)}) collective-permute-start(bf16[16,2048]{1,0:T(8,128)(2,1)} %convert_element_type.147), channel_id=1, source_target_pairs={{0,0},{1,8},{2,16},{3,24},{4,32},{5,40},{6,48},{7,56},{8,64},{9,72... | collective-permute-start | bytes 196616 | tf_op jit(solution)/shard_map/ppermute | solution.py:986
  71.8 1.1 slice.117
  73.5 1.3 slice_reduce_fusion.1
  78.2 3.4 fusion.22
  81.6 1.9 dynamic-slice_cosine_fusion.c_ref
  83.6 4.8 %fusion = (f32[2,1024,128]{2,1,0:T(8,128)S(1)}, f32[2,1024,128]{2,1,0:T(8,128)S(1)}, f32[2,1024,128]{2,1,0:T(8,128)}) fusion(f32[128]{0:T(128)S(1)} %reshape.334, f32[2,1024]{1,0:T(2,128)S(1)} %fusion.25, pred[128]{0:T(512)(128)(4,1)S(1)} %copy-done.70), kind=kLoop, calls=%fused_computation.4 | loop fusion | flops 1048576 | bytes 3154560 | tf_op jit(solution)/shard_map/jit(_where)/select_n | solution.py:82
  88.4 6.0 %shard_map.384 = (bf16[1024,2048]{1,0:T(8,128)(2,1)S(1)}, bf16[1024,768]{1,0:T(8,128)(2,1)S(1)}) custom-call(bf16[1024,2048]{1,0:T(8,128)(2,1)} %bitcast.132, bf16[2048,896]{1,0:T(8,128)(2,1)S(1)} %bitcast.130, f32[1,2048]{1,0:T(1,128)S(1)} %slice.96.gain_ref, f32[1,2048]{1,0:T(1,128)S(1)} %slice.98.shift_ref, f32[1,768]{1,0:T(1,128)S(1)} %reshape.308.bias_ref, ...), custom_call_target="tpu_custom_call" | custom-call | flops 3221225472 | bytes 14680064 | tf_op jit(solution)/shard_map/pallas_call | solution.py:570
  94.5 1.1 copy-done.9
  95.6 2.0 copy-done.36
  98.5 1.4 copy-done.10
  99.9 48.0 %shard_map.385 = (bf16[1024,256]{1,0:T(8,128)(2,1)S(1)}, f32[2,128,1024]{2,1,0:T(8,128)S(1)}, f32[2,8,1024]{2,1,0:T(8,128)S(1)}, bf16[2,1024,384]{2,1,0:T(8,128)...) custom-call(s32[1,1]{1,0:T(1,128)} %bitcast.11.refs_0_, ...), custom_call_target="tpu_custom_call" | custom-call | bytes 157941760 | tf_op jit(solution)/shard_map/pallas_call | solution.py:533
  148.0 1.2 copy-done.11
  149.1 1.0 copy-done.15
  150.8 2.0 copy-done.28
  152.7 1.3 convolution_convert_fusion
  154.0 26.1 %shard_map.386 = (f32[128,2048]{1,0:T(8,128)S(1)}, bf16[4,4,128,768]{3,2,1,0:T(8,128)(2,1)S(1)}) custom-call(bf16[8,128,2048]{2,1,0:T(8,128)(2,1)S(1)} %bitcast.116, bf16[128,768]{1,0:T(8,128)(2,1)S(1)} %get-tuple-element.129.refs_1_), custom_call_target="tpu_custom_call" | custom-call | bytes 73400320 | tf_op jit(solution)/shard_map/pallas_call | solution.py:533
  180.1 1.2 fusion.46
  181.4 1.6 multiply_reduce_fusion.2
  183.0 1.5 add_convert_fusion.1.refs_0_
  184.5 27.1 %shard_map.387 = (bf16[8,128,2048]{2,1,0:T(8,128)(2,1)S(1)}, bf16[4,4,48,2048]{3,2,1,0:T(8,128)(2,1)S(1)}) custom-call(bf16[128,2048]{1,0:T(8,128)(2,1)S(1)} %add_convert_fusion.1.refs_0_, bf16[48,2048]{1,0:T(8,128)(2,1)S(1)} %pad.27.refs_1_), custom_call_target="tpu_custom_call" | custom-call | bytes 146800640 | tf_op jit(solution)/shard_map/pallas_call | solution.py:533
  211.7 1.9 copy-done.30
  213.6 1.7 copy-done.33
  215.3 28.0 %shard_map.388 = (bf16[1024,768]{1,0:T(8,128)(2,1)}, bf16[1024,768]{1,0:T(8,128)(2,1)}, bf16[1024,768]{1,0:T(8,128)(2,1)}, bf16[1024,2048]{1,0:T(8,128)(2,1)}, bf16[1024,2048]{1,0:T(8,128)(2,1)}) custom-call(bf16[1024,2048]{1,0:T(8,128)(2,1)} %bitcast.138, bf16[1024,2048]{1,0:T(8,128)(2,1)} %bitcast.136, ...), custom_call_target="tpu_custom_call" | custom-call | flops 19327352832 | bytes 31457280 | tf_op jit(solution)/shard_map/pallas_call | solution.py:839
  243.3 1.4 copy-done.38
  244.7 4.0 shard_map.389
  248.7 25.9 %shard_map.390 = (f32[128,2048]{1,0:T(8,128)S(1)}, bf16[48,2048]{1,0:T(8,128)(2,1)S(1)}) custom-call(bf16[8,128,2048]{2,1,0:T(8,128)(2,1)S(1)} %bitcast.117, bf16[4,4,48,2048]{3,2,1,0:T(8,128)(2,1)S(1)} %bitcast.120), custom_call_target="tpu_custom_call" | custom-call | bytes 14417920 | tf_op jit(solution)/shard_map/pallas_call | solution.py:533
  274.6 2.2 multiply_reduce_fusion
  276.8 7.7 %shard_map.391 = (bf16[2048,768]{1,0:T(8,128)(2,1)S(1)}, bf16[2048,768]{1,0:T(8,128)(2,1)S(1)}) custom-call(bf16[1024,2048]{1,0:T(8,128)(2,1)S(1)} %bitcast.139, bf16[1024,768]{1,0:T(8,128)(2,1)S(1)} %copy-done.39, bf16[1024,768]{1,0:T(8,128)(2,1)S(1)} %copy-done.40), custom_call_target="tpu_custom_call" | custom-call | flops 6442450944 | bytes 12582912 | tf_op jit(solution)/shard_map/pallas_call | solution.py:865
  284.5 1.6 copy-done.5
  286.1 1.6 copy-done.6
  287.8 3.1 fusion.45
  290.9 28.1 %shard_map.392 = (bf16[8,128,2048]{2,1,0:T(8,128)(2,1)S(1)}, bf16[128,768]{1,0:T(8,128)(2,1)S(1)}) custom-call(bf16[128,2048]{1,0:T(8,128)(2,1)S(1)} %get-tuple-element.118.refs_0_, bf16[4,4,128,768]{3,2,1,0:T(8,128)(2,1)S(1)} %bitcast.121), custom_call_target="tpu_custom_call" | custom-call | bytes 87818240 | tf_op jit(solution)/shard_map/pallas_call | solution.py:533
  319.1 1.3 convolution_convert_fusion.2.refs_2_
  321.2 1.6 copy-done.1
  323.9 45.4 %shard_map.393 = (bf16[1024,768]{1,0:T(8,128)(2,1)S(1)}, f32[128,2048]{1,0:T(8,128)S(1)}) custom-call(s32[1,1]{1,0:T(1,128)} %bitcast.11.refs_0_, bf16[2,1024,384]{2,1,0:T(8,128)(2,1)S(1)} %copy-done.12, bf16[1024,256]{1,0:T(8,128)(2,1)S(1)} %convolution_convert_fusion.2.refs_2_, f32[2,128,1024]{2,1,0:T(8,128)S(1)} %copy-done.16, ...), custom_call_target="tpu_custom_call" | custom-call | bytes 41943040 | tf_op jit(solution)/shard_map/pallas_call | solution.py:533
  369.3 6.2 %shard_map.394 = (bf16[1024,2048]{1,0:T(8,128)(2,1)S(1)}, f32[8,2048]{1,0:T(8,128)S(1)}, f32[8,768]{1,0:T(8,128)S(1)}) custom-call(bf16[1024,768]{1,0:T(8,128)(2,1)S(1)} %get-tuple-element.78.dx_ref.refs_0_, bf16[1024,2048]{1,0:T(8,128)(2,1)S(1)} %bitcast.133, bf16[2048,896]{1,0:T(8,128)(2,1)S(1)} %bitcast.131), custom_call_target="tpu_custom_call" | custom-call | flops 3221225472 | bytes 14680064 | tf_op jit(solution)/shard_map/pallas_call | solution.py:895
  375.5 2.0 copy-done.2
  378.6 1.4 copy-done.35
  380.0 2.2 copy-done.37
  382.2 4.5 shard_map.395
  386.8 1.3 convolution_convert_fusion.1
  388.0 0.9 copy-done.3
  388.9 33.5 %shard_map.396 = (f32[128,2048]{1,0:T(8,128)S(1)}, bf16[128,768]{1,0:T(8,128)(2,1)S(1)}, bf16[16,2048]{1,0:T(8,128)(2,1)S(1)}, bf16[16,512]{1,0:T(8,128)(2,1)S(1)}) custom-call(bf16[8,128,2048]{2,1,0:T(8,128)(2,1)S(1)} %bitcast.119, bf16[4,4,128,768]{3,2,1,0:T(8,128)(2,1)S(1)} %bitcast.122, bf16[4,4,16,2048]{3,2,1,0:T(8,128)(2,1)S(1)} %bitcast.127, ...), custom_call_target="tpu_custom_call" | custom-call | bytes 16056320 | tf_op jit(solution)/shard_map/pallas_call | solution.py:533
  422.5 6.8 %collective-permute-start.1 = (bf16[16,2048]{1,0:T(8,128)(2,1)S(1)}, bf16[16,2048]{1,0:T(8,128)(2,1)}, u32[]{:S(2)}, u32[]{:S(2)}) collective-permute-start(bf16[16,2048]{1,0:T(8,128)(2,1)S(1)} %get-tuple-element.87), channel_id=1, source_target_pairs={{0,0},{8,1},{16,2},{24,3},{32,4},{40,5},{48,6},{56,7},{64,8},{72,9... | collective-permute-start | bytes 196616 | tf_op jit(solution)/shard_map/ppermute | solution.py:1068
  429.8 2.4 multiply_subtract_fusion
  432.3 2.2 fusion.16
  434.5 1.5 fusion.13
  436.6 1.6 multiply_subtract_fusion.4
  438.3 1.0 pad_maximum_fusion
  439.2 11.3 %shard_map.397 = bf16[8,16,2304]{2,1,0:T(8,128)(2,1)S(1)} custom-call(bf16[8,16,2304]{2,1,0:T(8,128)(2,1)S(1)} %bitcast.123), custom_call_target="tpu_custom_call" | custom-call | bytes 11796480 | tf_op jit(solution)/shard_map/pallas_call | solution.py:533
  451.9 1.3 reshape.337
  454.7 1.3 reshape.336
  456.8 2.3 multiply_subtract_fusion.2
  459.1 2.2 multiply_subtract_fusion.3
  461.4 1.2 multiply_subtract_fusion.1
  (214 shorter events, 16.8 us)
Async XLA Ops:
  7.2 10.0 %copy-start.41 = (bf16[1,128,2048]{2,1,0:T(8,128)(2,1)S(1)}, bf16[1,128,2048]{2,1,0:T(8,128)(2,1)}, u32[]{:S(2)}) copy-start(bf16[1,128,2048]{2,1,0:T(8,128)(2,1)} %param.24) | copy-start | bytes 1572868
  7.2 10.3 %copy-start.49 = (f32[16,5632]{1,0:T(8,128)S(1)}, f32[16,5632]{1,0:T(8,128)}, u32[]{:S(2)}) copy-start(f32[16,5632]{1,0:T(8,128)} %param.34) | copy-start | bytes 1081348
  7.2 208.1 %all-gather.2.cloned.1.call-start = ((), (), s32[]{:S(2)}) async-start(), calls=%async_computation.1 | async-start | bytes 3342336 | tf_op jit(solution)/shard_map/all_gather | solution.py:967
  14.0 5.7 %copy-start.47 = (f32[16,5632]{1,0:T(8,128)S(1)}, f32[16,5632]{1,0:T(8,128)}, u32[]{:S(2)}) copy-start(f32[16,5632]{1,0:T(8,128)} %param.37) | copy-start | bytes 1081348
  21.2 42.5 %copy-start.52 = (f32[16,2048]{1,0:T(8,128)S(1)}, f32[16,2048]{1,0:T(8,128)}, u32[]{:S(2)}) copy-start(f32[16,2048]{1,0:T(8,128)} %param.31) | copy-start | bytes 393220
  21.3 51.8 %copy-start.71 = (pred[16,8]{1,0:T(8,128)(4,1)S(1)}, pred[16,8]{1,0:T(8,128)(4,1)}, u32[]{:S(2)}) copy-start(pred[16,8]{1,0:T(8,128)(4,1)} %constant.203) | copy-start | bytes 388
  59.1 1.8 copy-start.19
  60.9 2.0 copy-start.24
  63.6 374.7 %reduce-scatter.2.cloned.1.call-start = ((), (), s32[]{:S(2)}) async-start(), calls=%async_computation.2 | async-start | bytes 3342336 | tf_op jit(solution)/shard_map/reduce_scatter | solution.py:1018
  64.3 34.2 %collective-permute-start = (bf16[16,2048]{1,0:T(8,128)(2,1)}, bf16[16,2048]{1,0:T(8,128)(2,1)S(1)}, u32[]{:S(2)}, u32[]{:S(2)}) collective-permute-start(bf16[16,2048]{1,0:T(8,128)(2,1)} %convert_element_type.147), channel_id=1, source_target_pairs={{0,0},{1,8},{2,16},{3,24},{4,32},{5,40},{6,48},{7,56},{8,64},{9,72... | collective-permute-start | bytes 196616 | tf_op jit(solution)/shard_map/ppermute | solution.py:986
  72.9 10.6 %copy-start.70 = (pred[128]{0:T(512)(128)(4,1)S(1)}, pred[128]{0:T(512)(128)(4,1)}, u32[]{:S(2)}) copy-start(pred[128]{0:T(512)(128)(4,1)} %constant.168.clone) | copy-start | bytes 388
  81.6 6.8 %copy-start.20 = (bf16[4,4,128,896]{3,2,1,0:T(8,128)(2,1)S(1)}, bf16[4,4,128,896]{3,2,1,0:T(8,128)(2,1)}, u32[]{:S(2)}) copy-start(bf16[4,4,128,896]{3,2,1,0:T(8,128)(2,1)} %copy-done.19) | copy-start | bytes 11010052
  88.4 9.2 %copy-start.57 = (f32[128,16]{1,0:T(8,128)S(1)}, f32[128,16]{1,0:T(8,128)}, u32[]{:S(2)}) copy-start(f32[128,16]{1,0:T(8,128)} %get-tuple-element.96) | copy-start | bytes 24580
  88.4 9.3 %copy-start.56 = (f32[128,16]{1,0:T(8,128)S(1)}, f32[128,16]{1,0:T(8,128)}, u32[]{:S(2)}) copy-start(f32[128,16]{1,0:T(8,128)} %get-tuple-element.98) | copy-start | bytes 24580
  88.4 10.0 %copy-start.45 = (f32[44,2048]{1,0:T(8,128)S(1)}, f32[44,2048]{1,0:T(8,128)}, u32[]{:S(2)}) copy-start(f32[44,2048]{1,0:T(8,128)} %param.40) | copy-start | bytes 1081348
  88.4 10.1 %copy-start.8 = (bf16[1,128,2048]{2,1,0:T(8,128)(2,1)S(1)}, bf16[1,128,2048]{2,1,0:T(8,128)(2,1)}, u32[]{:S(2)}) copy-start(bf16[1,128,2048]{2,1,0:T(8,128)(2,1)} %param.25) | copy-start | bytes 1572868
  95.6 2.0 copy-start.36
  150.8 2.0 copy-start.28
  154.0 26.1 %copy-start.42 = (bf16[1,128,2048]{2,1,0:T(8,128)(2,1)S(1)}, bf16[1,128,2048]{2,1,0:T(8,128)(2,1)}, u32[]{:S(2)}) copy-start(bf16[1,128,2048]{2,1,0:T(8,128)(2,1)} %param.24) | copy-start | bytes 1572868
  154.0 29.0 %copy-start.60 = (f32[2048]{0:T(1024)S(1)}, f32[2048]{0:T(1024)}, u32[]{:S(2)}) copy-start(f32[2048]{0:T(1024)} %add.222) | copy-start | bytes 24580
  180.1 2.9 copy-start.32
  211.7 1.9 copy-start.30
  213.6 1.7 copy-start.33
  215.3 28.0 %copy-start.29 = (bf16[8,128,2048]{2,1,0:T(8,128)(2,1)S(1)}, bf16[8,128,2048]{2,1,0:T(8,128)(2,1)}, u32[]{:S(2)}) copy-start(bf16[8,128,2048]{2,1,0:T(8,128)(2,1)} %copy-done.28) | copy-start | bytes 12582916
  244.7 4.0 copy-start
  248.7 28.2 %copy-start.31 = (bf16[8,128,2048]{2,1,0:T(8,128)(2,1)S(1)}, bf16[8,128,2048]{2,1,0:T(8,128)(2,1)}, u32[]{:S(2)}) copy-start(bf16[8,128,2048]{2,1,0:T(8,128)(2,1)} %copy-done.30) | copy-start | bytes 12582916
  248.7 28.2 %copy-start.39 = (bf16[1024,768]{1,0:T(8,128)(2,1)S(1)}, bf16[1024,768]{1,0:T(8,128)(2,1)}, u32[]{:S(2)}) copy-start(bf16[1024,768]{1,0:T(8,128)(2,1)} %get-tuple-element.70.refs_0_) | copy-start | bytes 4718596
  248.7 28.2 %copy-start.40 = (bf16[1024,768]{1,0:T(8,128)(2,1)S(1)}, bf16[1024,768]{1,0:T(8,128)(2,1)}, u32[]{:S(2)}) copy-start(bf16[1024,768]{1,0:T(8,128)(2,1)} %get-tuple-element.71.refs_1_) | copy-start | bytes 4718596
  286.1 1.6 copy-start.6
  287.8 3.1 copy-start.7
  287.8 31.2 %copy-start.18 = (bf16[4,4,16,2048]{3,2,1,0:T(8,128)(2,1)S(1)}, bf16[4,4,16,2048]{3,2,1,0:T(8,128)(2,1)}, u32[]{:S(2)}) copy-start(bf16[4,4,16,2048]{3,2,1,0:T(8,128)(2,1)} %copy-done.17) | copy-start | bytes 3145732
  319.0 2.2 copy-start.26
  319.0 3.8 copy-start.1
  319.0 4.1 copy-start.4
  319.0 4.6 copy-start.12
  319.1 4.8 %copy-start.16 = (f32[2,128,1024]{2,1,0:T(8,128)S(1)}, f32[2,128,1024]{2,1,0:T(8,128)}, u32[]{:S(2)}) copy-start(f32[2,128,1024]{2,1,0:T(8,128)} %copy-done.15) | copy-start | bytes 3145732
  319.1 4.8 %copy-start.23 = (f32[2,8,1024]{2,1,0:T(8,128)S(1)}, f32[2,8,1024]{2,1,0:T(8,128)}, u32[]{:S(2)}) copy-start(f32[2,8,1024]{2,1,0:T(8,128)} %copy-done.22) | copy-start | bytes 196612
  323.9 45.4 %copy-start.21 = (bf16[4,4,128,896]{3,2,1,0:T(8,128)(2,1)S(1)}, bf16[4,4,128,896]{3,2,1,0:T(8,128)(2,1)}, u32[]{:S(2)}) copy-start(bf16[4,4,128,896]{3,2,1,0:T(8,128)(2,1)} %copy-done.19) | copy-start | bytes 11010052
  323.9 45.4 %copy-start.25 = (bf16[8,128,2048]{2,1,0:T(8,128)(2,1)S(1)}, bf16[8,128,2048]{2,1,0:T(8,128)(2,1)}, u32[]{:S(2)}) copy-start(bf16[8,128,2048]{2,1,0:T(8,128)(2,1)} %copy-done.24) | copy-start | bytes 12582916
  369.3 6.2 %copy-start.34 = (bf16[1024,768]{1,0:T(8,128)(2,1)}, bf16[1024,768]{1,0:T(8,128)(2,1)S(1)}, u32[]{:S(2)}) copy-start(bf16[1024,768]{1,0:T(8,128)(2,1)S(1)} %get-tuple-element.78.dx_ref.refs_0_) | copy-start | bytes 4718596
  369.3 8.5 %copy-start.62 = (bf16[2048]{0:T(1024)(128)(2,1)S(1)}, bf16[2048]{0:T(1024)(128)(2,1)}, u32[]{:S(2)}) copy-start(bf16[2048]{0:T(1024)(128)(2,1)} %get-tuple-element.90) | copy-start | bytes 12292
  369.3 8.6 %copy-start.61 = (bf16[2048]{0:T(1024)(128)(2,1)S(1)}, bf16[2048]{0:T(1024)(128)(2,1)}, u32[]{:S(2)}) copy-start(bf16[2048]{0:T(1024)(128)(2,1)} %get-tuple-element.95) | copy-start | bytes 12292
  375.5 2.0 copy-start.2
  380.0 2.2 copy-start.37
  382.2 4.5 copy-start.14
  382.2 4.5 copy-start.27
  386.8 2.2 copy-start.3
  388.9 40.5 %copy-start.43 = (bf16[1,128,2048]{2,1,0:T(8,128)(2,1)S(1)}, bf16[1,128,2048]{2,1,0:T(8,128)(2,1)}, u32[]{:S(2)}) copy-start(bf16[1,128,2048]{2,1,0:T(8,128)(2,1)} %param.24) | copy-start | bytes 1572868
  388.9 40.5 %copy-start.65 = (f32[128]{0:T(128)S(1)}, f32[128]{0:T(128)}, u32[]{:S(2)}) copy-start(f32[128]{0:T(128)} %copy-done.64) | copy-start | bytes 1540
  388.9 40.5 %copy-start.67 = (f32[128]{0:T(128)S(1)}, f32[128]{0:T(128)}, u32[]{:S(2)}) copy-start(f32[128]{0:T(128)} %copy-done.66) | copy-start | bytes 1540
  422.5 14.1 %collective-permute-start.1 = (bf16[16,2048]{1,0:T(8,128)(2,1)S(1)}, bf16[16,2048]{1,0:T(8,128)(2,1)}, u32[]{:S(2)}, u32[]{:S(2)}) collective-permute-start(bf16[16,2048]{1,0:T(8,128)(2,1)S(1)} %get-tuple-element.87), channel_id=1, source_target_pairs={{0,0},{8,1},{16,2},{24,3},{32,4},{40,5},{48,6},{56,7},{64,8},{72,9... | collective-permute-start | bytes 196616 | tf_op jit(solution)/shard_map/ppermute | solution.py:1068
  429.5 5.1 %copy-start.44 = (f32[128,2048]{1,0:T(8,128)S(1)}, f32[128,2048]{1,0:T(8,128)}, u32[]{:S(2)}) copy-start(f32[128,2048]{1,0:T(8,128)} %get-tuple-element.119) | copy-start | bytes 3145732
  432.3 3.7 copy-start.63
  432.3 3.7 copy-start.68
  432.3 3.7 copy-start.69
  432.3 4.3 copy-start.53
  432.3 4.3 copy-start.58
  432.3 4.3 copy-start.59
  454.0 2.8 copy-start.48
  454.6 4.5 copy-start.50
  456.0 3.1 copy-start.51
  456.4 4.9 %copy-start.46 = (f32[16,6144]{1,0:T(8,128)S(1)}, f32[16,6144]{1,0:T(8,128)}, u32[]{:S(2)}) copy-start(f32[16,6144]{1,0:T(8,128)} %param.28) | copy-start | bytes 1179652
  456.4 4.9 %copy-start.54 = (f32[16,6144]{1,0:T(8,128)S(1)}, f32[16,6144]{1,0:T(8,128)}, u32[]{:S(2)}) copy-start(f32[16,6144]{1,0:T(8,128)} %param.29) | copy-start | bytes 1179652
  456.4 4.9 %copy-start.55 = (f32[16,6144]{1,0:T(8,128)S(1)}, f32[16,6144]{1,0:T(8,128)}, u32[]{:S(2)}) copy-start(f32[16,6144]{1,0:T(8,128)} %param.30) | copy-start | bytes 1179652
  (12 other events, 14.2 us)
Sparse Core Ops, SparseCore 0:
  63.7 55.4 all-gather.1
  287.9 76.3 reduce-scatter.1
